TPU v7x, 512 devices: a whole 4x8x8 slice. The times are simulated.
512 devices in a mesh: leaf: 64 (over z, x, core), panel: 8 (over y).
Axes of the slice: x: 4, y: 8, z: 8, core: 2. Of those that a mesh axis runs over, the one named last changes fastest.
Arguments:
- inverse_root: bfloat16 [2, 5120, 5120], P(None, 'panel', 'leaf'), may hold values from -0.0625 to 0.0625
- inverse_upper: bfloat16 [2, 5120, 10240], P(None, 'panel', 'leaf'), may hold values from -0.0625 to 0.0625
- inverse_middle: bfloat16 [2, 5120, 20480], P(None, 'panel', 'leaf'), may hold values from -0.0625 to 0.0625
- inverse_lower: bfloat16 [2, 5120, 40960], P(None, 'panel', 'leaf'), may hold values from -0.0625 to 0.0625
- coupling_upper: bfloat16 [2, 5120, 5120], P(None, 'leaf', 'panel'), may hold values from -0.0625 to 0.0625
- coupling_middle: bfloat16 [2, 10240, 5120], P(None, 'leaf', 'panel'), may hold values from -0.0625 to 0.0625
- coupling_lower: bfloat16 [2, 20480, 5120], P(None, 'leaf', 'panel'), may hold values from -0.0625 to 0.0625
- source_root: bfloat16 [2, 64, 5120], P(None, 'panel', 'leaf'), may hold values from -6 to 6
- source_upper: bfloat16 [2, 64, 10240], P(None, 'panel', 'leaf'), may hold values from -6 to 6
- source_middle: bfloat16 [2, 64, 20480], P(None, 'panel', 'leaf'), may hold values from -6 to 6
- source_lower: bfloat16 [2, 64, 40960], P(None, 'panel', 'leaf'), may hold values from -6 to 6
- blocks_upper: int32 [2, 20], replicated, may hold values from 0 to 39, as said below
- blocks_middle: int32 [4, 20], replicated, may hold values from 0 to 59, as said below
- blocks_lower: int32 [8, 20], replicated, may hold values from 0 to 59, as said below
- live_blocks: int32 [15], replicated, may hold values from 20 to 40, as said below
Outputs:
- answer_root: float32 [2, 64, 5120], P(None, 'panel', 'leaf')
- answer_upper: float32 [2, 64, 10240], P(None, 'panel', 'leaf')
- answer_middle: float32 [2, 64, 20480], P(None, 'panel', 'leaf')
- answer_lower: float32 [2, 64, 40960], P(None, 'panel', 'leaf')
Inputs may be any that keep to these rules, and one draw needn't show every extreme that they name: `blocks_upper`: row f names 20 distinct blocks of the parent's front, whose blocks are the root's 40 pivot blocks; some row names the parent's first and last block. `blocks_middle`: row f names 20 distinct blocks of the parent's front (40 pivot blocks, then 20 update blocks); some row names the parent's first and last block. `blocks_lower`: row f names 20 distinct blocks of the parent's front (40 pivot blocks, then 20 update blocks); some row names the parent's first and last block. `live_blocks`: entry 2**l - 1 + f belongs to front f of level l; the root's entry is 40, and one front of level 3 has half of 40.
All inputs are finite; a program needn't handle non-finite values.
Results may differ from a plain program's by a relative error of at most 0.035.
Values may be sent and summed in bfloat16 or wider, within the bound.
No kernel may reach another device: no remote copies, remote signals or barrier semaphores. Data moves between devices by JAX's collectives and lax.ppermute only.
A program may use at most 128 MiB of HBM per device.

v0:
```python
import jax
import jax.numpy as jnp
from jax import lax
from jax.sharding import PartitionSpec as P

BLOCK = 128
P_SIZE = 5120
U = 2560


PAIR_DIMS = (((1,), (1,)), ((), ()))
FLAT_DIMS = (((1,), (0,)), ((), ()))


def partner(value, axis, apart):
    mask = 2**apart
    pairs = [(source, source ^ mask) for source in range(lax.axis_size(axis))]
    return lax.ppermute(value, axis, pairs)


def conj_apply(matrix, vector):
    real_one = lax.dot_general(vector[0], matrix[0], PAIR_DIMS, preferred_element_type=jnp.float32)
    real_two = lax.dot_general(vector[1], matrix[1], PAIR_DIMS, preferred_element_type=jnp.float32)
    imag_one = lax.dot_general(vector[1], matrix[0], PAIR_DIMS, preferred_element_type=jnp.float32)
    imag_two = lax.dot_general(vector[0], matrix[1], PAIR_DIMS, preferred_element_type=jnp.float32)
    return jnp.stack([real_one + real_two, imag_one - imag_two])


def herm_apply(matrix, vector):
    real_one = lax.dot_general(vector[0], matrix[0], FLAT_DIMS, preferred_element_type=jnp.float32)
    real_two = lax.dot_general(vector[1], matrix[1], FLAT_DIMS, preferred_element_type=jnp.float32)
    imag_one = lax.dot_general(vector[1], matrix[0], FLAT_DIMS, preferred_element_type=jnp.float32)
    imag_two = lax.dot_general(vector[0], matrix[1], FLAT_DIMS, preferred_element_type=jnp.float32)
    return jnp.stack([real_one + real_two, imag_one - imag_two])


def live_mask(live_blocks, slot_index, row_start, row_count):
    live_count = lax.dynamic_slice_in_dim(live_blocks, slot_index, 1, 0)[0]
    row_ids = row_start + jnp.arange(row_count, dtype=jnp.int32)
    return (row_ids // BLOCK < live_count).astype(jnp.float32)


def pair_sums(partial_value, bit_count):
    summed = partial_value
    for bit_number in range(bit_count):
        summed = summed + partner(summed.astype(jnp.bfloat16), "leaf", bit_number).astype(
            summed.dtype
        )
    return summed


def group_total(partial_value, group_width):
    bit_count = group_width.bit_length() - 1
    return pair_sums(partial_value, bit_count)


def level_gather(section):
    return lax.all_gather(section, "leaf", axis=2, tiled=True)


def full_columns(section):
    return lax.all_gather(section, "panel", axis=1, tiled=True)


def panel_shares(partial_value):
    return lax.psum_scatter(
        partial_value.astype(jnp.bfloat16), "panel", scatter_dimension=1, tiled=True
    ).astype(jnp.float32)


def shards(
    inverse_root,
    inverse_upper,
    inverse_middle,
    inverse_lower,
    coupling_upper,
    coupling_middle,
    coupling_lower,
    source_root,
    source_upper,
    source_middle,
    source_lower,
    blocks_upper,
    blocks_middle,
    blocks_lower,
    live_blocks,
):
    inverses = (inverse_root, inverse_upper, inverse_middle, inverse_lower)
    couplings = (None, coupling_upper, coupling_middle, coupling_lower)
    sources = (source_root, source_upper, source_middle, source_lower)
    tables = (None, blocks_upper, blocks_middle, blocks_lower)
    leaves = lax.axis_size("leaf")
    panels = lax.axis_size("panel")
    position = lax.axis_index("leaf")
    column = lax.axis_index("panel")
    rhs_split = source_lower.shape[1]
    panel_rows = P_SIZE // panels
    update_blocks = U // BLOCK
    solved = [None, None, None, None]
    gathered = None
    for level_index in (3, 2, 1, 0):
        group_width = leaves >> level_index
        front_index = position // group_width
        within = position % group_width
        slot_index = (1 << level_index) - 1 + front_index
        own_rows = P_SIZE // group_width
        own_updates = U // group_width
        pivot_mask = live_mask(live_blocks, slot_index, within * own_rows, own_rows)
        source = sources[level_index].astype(jnp.float32)
        passed = None
        if level_index == 3:
            reduced = source * pivot_mask
        else:
            block_count = P_SIZE // BLOCK + (update_blocks if level_index >= 1 else 0)
            child_pair = lax.dynamic_slice_in_dim(tables[level_index + 1], 2 * front_index, 2, 0)
            children = lax.dynamic_slice_in_dim(gathered, 2 * front_index * U, 2 * U, 2)
            child_blocks = children.astype(jnp.float32).reshape(
                2, rhs_split, 2, update_blocks, BLOCK
            )
            select = (
                child_pair[:, :, None] == jnp.arange(block_count, dtype=jnp.int32)[None, None, :]
            ).astype(jnp.float32)
            assembled = jnp.einsum(
                "crhbx,hbk->crkx", child_blocks, select, precision=lax.Precision.HIGHEST
            )
            assembled = assembled.reshape(2, rhs_split, block_count * BLOCK)
            reduced = (
                source - lax.dynamic_slice_in_dim(assembled, within * own_rows, own_rows, 2)
            ) * pivot_mask
            if level_index >= 1:
                passed = lax.dynamic_slice_in_dim(
                    assembled, P_SIZE + within * own_updates, own_updates, 2
                )
        forward_input = full_columns(reduced.astype(jnp.bfloat16))
        summed = group_total(conj_apply(inverses[level_index], forward_input), group_width)
        row_mask = live_mask(live_blocks, slot_index, column * panel_rows, panel_rows)
        solved_rows = (summed * row_mask).astype(jnp.bfloat16)
        solved[level_index] = solved_rows
        if level_index >= 1:
            update = panel_shares(conj_apply(couplings[level_index], solved_rows))
            if passed is not None:
                update = update + passed
            gathered = level_gather(update.astype(jnp.bfloat16))
    answers = [None, None, None, None]
    joined = None
    for level_index in (0, 1, 2, 3):
        group_width = leaves >> level_index
        front_index = position // group_width
        within = position % group_width
        slot_index = (1 << level_index) - 1 + front_index
        own_rows = P_SIZE // group_width
        own_updates = U // group_width
        pivot_mask = live_mask(live_blocks, slot_index, within * own_rows, own_rows)
        update_split = None
        if level_index == 0:
            target = solved[0]
        else:
            prev_width = group_width * 2
            piece_rows = P_SIZE // prev_width + (U // prev_width if level_index >= 2 else 0)
            every_block = joined.reshape(2, rhs_split, leaves // prev_width, prev_width, piece_rows)
            parent_block = lax.dynamic_slice_in_dim(every_block, front_index // 2, 1, 2)[:, :, 0]
            pivot_part = parent_block[:, :, :, : P_SIZE // prev_width].reshape(2, rhs_split, P_SIZE)
            if level_index >= 2:
                upper_part = parent_block[:, :, :, P_SIZE // prev_width :].reshape(2, rhs_split, U)
                front_values = jnp.concatenate([pivot_part, upper_part], 2)
            else:
                front_values = pivot_part
            block_count = front_values.shape[2] // BLOCK
            map_row = lax.dynamic_slice_in_dim(tables[level_index], front_index, 1, 0)[0]
            select = (map_row[:, None] == jnp.arange(block_count, dtype=jnp.int32)[None, :]).astype(
                jnp.float32
            )
            picked = jnp.einsum(
                "crkx,bk->crbx",
                front_values.astype(jnp.float32).reshape(2, rhs_split, block_count, BLOCK),
                select,
                precision=lax.Precision.HIGHEST,
            )
            picked = picked.reshape(2, rhs_split, U)
            update_split = lax.dynamic_slice_in_dim(
                picked, within * own_updates, own_updates, 2
            ).astype(jnp.bfloat16)
            update_full = full_columns(update_split)
            correction = group_total(herm_apply(couplings[level_index], update_full), group_width)
            target = (solved[level_index].astype(jnp.float32) - correction).astype(jnp.bfloat16)
        answer = panel_shares(herm_apply(inverses[level_index], target)) * pivot_mask
        answers[level_index] = answer
        if level_index < 3:
            outgoing_values = answer.astype(jnp.bfloat16)
            if update_split is not None:
                outgoing_values = jnp.concatenate([outgoing_values, update_split], 2)
            joined = level_gather(outgoing_values)
    return (answers[0], answers[1], answers[2], answers[3])


def solution(mesh):
    placed = (
        P(None, "panel", "leaf"),
        P(None, "panel", "leaf"),
        P(None, "panel", "leaf"),
        P(None, "panel", "leaf"),
        P(None, "leaf", "panel"),
        P(None, "leaf", "panel"),
        P(None, "leaf", "panel"),
        P(None, "panel", "leaf"),
        P(None, "panel", "leaf"),
        P(None, "panel", "leaf"),
        P(None, "panel", "leaf"),
        P(),
        P(),
        P(),
        P(),
    )
    return jax.shard_map(
        shards,
        mesh=mesh,
        in_specs=placed,
        out_specs=(
            P(None, "panel", "leaf"),
            P(None, "panel", "leaf"),
            P(None, "panel", "leaf"),
            P(None, "panel", "leaf"),
        ),
        check_vma=False,
    )
```

profile of v0, /device:TPU:6, one launch (start us, length us, event | category | flops | bytes accessed | tf_op | source)
XLA Modules:
  0.0 1166.5 jit_solution(4107627424636204804)
XLA Ops:
  10.2 26.2 %all_gather.39 = bf16[2,64,640]{2,1,0:T(8,128)(2,1)S(1)} all-gather(bf16[2,8,640]{2,1,0:T(8,128)(2,1)S(1)} %multiply_convert_fusion.4), channel_id=1, replica_groups=mesh['leaf'=64,'panel'=8] {'panel'}, dimensions={1}, use_global_device_ids=true | all-gather | bytes 184320 | tf_op jit(solution)/shard_map/all_gather | solution.py:62
  63.6 79.1 %all-reduce.7.cloned.1.call-done = bf16[2,64,320]{2,1,0:T(8,128)(2,1)} async-done(((bf16[2,64,320]{2,1,0:T(8,128)(2,1)}), bf16[2,64,320]{2,1,0:T(8,128)(2,1)}) %all-reduce.7.cloned.1.call-update) | async-done | bytes 81936
  143.6 58.9 %all_gather.40 = bf16[2,8,20480]{1,0,2:T(2,128)(2,1)S(1)} all-gather(bf16[2,8,320]{1,0,2:T(2,128)(2,1)S(1)} %copy.43), channel_id=1, replica_groups=mesh['leaf'=64,'panel'=8] {'leaf'}, dimensions={2}, use_global_device_ids=true | all-gather | bytes 665600 | tf_op jit(solution)/shard_map/all_gather | solution.py:58
  212.9 24.7 %all_gather.41 = bf16[2,64,320]{2,1,0:T(8,128)(2,1)S(1)} all-gather(bf16[2,8,320]{2,1,0:T(8,128)(2,1)S(1)} %multiply_convert_fusion.5), channel_id=1, replica_groups=mesh['leaf'=64,'panel'=8] {'panel'}, dimensions={1}, use_global_device_ids=true | all-gather | bytes 92160 | tf_op jit(solution)/shard_map/all_gather | solution.py:62
  267.1 28.3 %all-reduce.1 = bf16[2,64,160]{2,1,0:T(8,128)(2,1)S(1)} all-reduce(bf16[2,64,160]{2,1,0:T(8,128)(2,1)S(1)} %pad_maximum_fusion.10), channel_id=3, replica_groups=mesh['leaf'=64,'panel'=8] {'panel'}, use_global_device_ids=true, to_apply=%region_1.2.clone | all-reduce | flops 20480 | bytes 81920
  296.4 51.9 %all_gather.42 = bf16[2,8,10240]{1,0,2:T(2,128)(2,1)S(1)} all-gather(bf16[2,8,160]{1,0,2:T(2,128)(2,1)S(1)} %copy.46), channel_id=1, replica_groups=mesh['leaf'=64,'panel'=8] {'leaf'}, dimensions={2}, use_global_device_ids=true | all-gather | bytes 332800 | tf_op jit(solution)/shard_map/all_gather | solution.py:58
  358.7 24.5 %all_gather.43 = bf16[2,64,160]{2,1,0:T(8,128)(2,1)S(1)} all-gather(bf16[2,8,160]{2,1,0:T(8,128)(2,1)S(1)} %multiply_convert_fusion.6), channel_id=1, replica_groups=mesh['leaf'=64,'panel'=8] {'panel'}, dimensions={1}, use_global_device_ids=true | all-gather | bytes 46080 | tf_op jit(solution)/shard_map/all_gather | solution.py:62
  424.9 35.0 %reduce-scatter.14.cloned.1.call-done = bf16[8,160]{1,0:T(8,128)(2,1)} async-done(((bf16[64,160]{1,0:T(8,128)(2,1)}), bf16[8,160]{1,0:T(8,128)(2,1)}) %reduce-scatter.14.cloned.1.call-update) | async-done | bytes 2576
  461.6 56.6 %all_gather.44 = bf16[2,8,5120]{1,0,2:T(2,128)(2,1)} all-gather(bf16[2,8,80]{1,0,2:T(2,128)(2,1)S(1)} %copy.49), channel_id=1, replica_groups=mesh['leaf'=64,'panel'=8] {'leaf'}, dimensions={2}, use_global_device_ids=true | all-gather | bytes 166400 | tf_op jit(solution)/shard_map/all_gather | solution.py:58
  526.4 21.5 %all_gather.45 = bf16[2,64,80]{2,1,0:T(8,128)(2,1)S(1)} all-gather(bf16[2,8,80]{2,1,0:T(8,128)(2,1)S(1)} %multiply_convert_fusion.7), channel_id=1, replica_groups=mesh['leaf'=64,'panel'=8] {'panel'}, dimensions={1}, use_global_device_ids=true | all-gather | bytes 23040 | tf_op jit(solution)/shard_map/all_gather | solution.py:62
  579.4 6.7 collective-permute-done.16
  593.1 7.3 collective-permute-done.17
  603.1 34.5 %reduce-scatter.16.cloned.1.call-done = bf16[8,160]{1,0:T(8,128)(2,1)} async-done(((bf16[64,160]{1,0:T(8,128)(2,1)}), bf16[8,160]{1,0:T(8,128)(2,1)}) %reduce-scatter.16.cloned.1.call-update) | async-done | bytes 2576
  639.1 56.6 %all_gather.46 = bf16[2,8,5120]{1,0,2:T(2,128)(2,1)} all-gather(bf16[2,8,80]{1,0,2:T(2,128)(2,1)S(1)} %copy.52), channel_id=1, replica_groups=mesh['leaf'=64,'panel'=8] {'leaf'}, dimensions={2}, use_global_device_ids=true | all-gather | bytes 166400 | tf_op jit(solution)/shard_map/all_gather | solution.py:58
  700.2 21.4 %all_gather.47 = bf16[2,64,80]{2,1,0:T(8,128)(2,1)S(1)} all-gather(bf16[2,8,80]{2,1,0:T(8,128)(2,1)S(1)} %dynamic-slice_convert_fusion.2), channel_id=1, replica_groups=mesh['leaf'=64,'panel'=8] {'panel'}, dimensions={1}, use_global_device_ids=true | all-gather | bytes 23040 | tf_op jit(solution)/shard_map/all_gather | solution.py:62
  753.9 6.0 collective-permute-done.22
  760.8 29.1 %all-reduce.2 = bf16[2,64,160]{2,1,0:T(8,128)(2,1)S(1)} all-reduce(bf16[2,64,160]{2,1,0:T(8,128)(2,1)S(1)} %pad_maximum_fusion.11), channel_id=6, replica_groups=mesh['leaf'=64,'panel'=8] {'panel'}, use_global_device_ids=true, to_apply=%region_4.5.clone | all-reduce | flops 20480 | bytes 81920
  791.4 54.1 %all_gather.48 = bf16[2,8,15360]{1,0,2:T(2,128)(2,1)S(1)} all-gather(bf16[2,8,240]{1,0,2:T(2,128)(2,1)} %copy.54), channel_id=1, replica_groups=mesh['leaf'=64,'panel'=8] {'leaf'}, dimensions={2}, use_global_device_ids=true | all-gather | bytes 499200 | tf_op jit(solution)/shard_map/all_gather | solution.py:58
  857.1 24.6 %all_gather.49 = bf16[2,64,160]{2,1,0:T(8,128)(2,1)S(1)} all-gather(bf16[2,8,160]{2,1,0:T(8,128)(2,1)S(1)} %dynamic-slice_convert_fusion.1), channel_id=1, replica_groups=mesh['leaf'=64,'panel'=8] {'panel'}, dimensions={1}, use_global_device_ids=true | all-gather | bytes 46080 | tf_op jit(solution)/shard_map/all_gather | solution.py:62
  914.7 73.8 %all-reduce.9.cloned.1.call-done = bf16[2,64,320]{2,1,0:T(8,128)(2,1)} async-done(((bf16[2,64,320]{2,1,0:T(8,128)(2,1)}), bf16[2,64,320]{2,1,0:T(8,128)(2,1)}) %all-reduce.9.cloned.1.call-update) | async-done | bytes 81936
  990.1 71.5 %all_gather.50 = bf16[2,8,30720]{1,0,2:T(2,128)(2,1)} all-gather(bf16[2,8,480]{1,0,2:T(2,128)(2,1)S(1)} %copy.57), channel_id=1, replica_groups=mesh['leaf'=64,'panel'=8] {'leaf'}, dimensions={2}, use_global_device_ids=true | all-gather | bytes 998400 | tf_op jit(solution)/shard_map/all_gather | solution.py:58
  1061.6 6.9 constant_dynamic-slice_fusion
  1075.3 24.7 %all_gather.51 = bf16[2,64,320]{2,1,0:T(8,128)(2,1)S(1)} all-gather(bf16[2,8,320]{2,1,0:T(8,128)(2,1)S(1)} %dynamic-slice_convert_fusion), channel_id=1, replica_groups=mesh['leaf'=64,'panel'=8] {'panel'}, dimensions={1}, use_global_device_ids=true | all-gather | bytes 92160 | tf_op jit(solution)/shard_map/all_gather | solution.py:62
  1123.3 35.0 %reduce-scatter.18.cloned.1.call-done = bf16[8,1280]{1,0:T(8,128)(2,1)} async-done(((bf16[64,1280]{1,0:T(8,128)(2,1)}), bf16[8,1280]{1,0:T(8,128)(2,1)}) %reduce-scatter.18.cloned.1.call-update) | async-done | bytes 20496
  (281 shorter events, 291.6 us)
Async XLA Ops:
  7.2 135.5 %all-reduce.7.cloned.1.call-start = ((), (), s32[]{:S(2)}) async-start(), calls=%async_computation.6 | async-start | bytes 196608
  43.6 8.1 collective-permute-start.1
  51.8 9.9 collective-permute-start.2
  63.5 396.4 %reduce-scatter.14.cloned.1.call-start = ((), (), s32[]{:S(2)}) async-start(), calls=%async_computation.3 | async-start | bytes 36864
  241.8 8.1 collective-permute-start.4
  250.0 8.8 collective-permute-start.5
  387.3 8.1 collective-permute-start.8
  395.5 8.8 collective-permute-start.9
  411.7 10.0 collective-permute-start.11
  424.2 213.4 %reduce-scatter.16.cloned.1.call-start = ((), (), s32[]{:S(2)}) async-start(), calls=%async_computation.4 | async-start | bytes 36864
  551.8 8.1 collective-permute-start.13
  560.0 8.8 collective-permute-start.14
  576.2 9.9 collective-permute-start.16
  587.5 13.0 %collective-permute-start.17 = (bf16[2,64,640]{2,1,0:T(8,128)(2,1)}, bf16[2,64,640]{2,1,0:T(8,128)(2,1)}, u32[]{:S(2)}, u32[]{:S(2)}) collective-permute-start(bf16[2,64,640]{2,1,0:T(8,128)(2,1)} %fusion.164), channel_id=1, source_target_pairs={{0,256},{8,264},{16,272},{24,280},{32,288},{40,296},{48,304},{56,3... | collective-permute-start | bytes 491528 | tf_op jit(solution)/shard_map/ppermute | solution.py:18
  603.0 385.5 %all-reduce.9.cloned.1.call-start = ((), (), s32[]{:S(2)}) async-start(), calls=%async_computation.7 | async-start | bytes 196608
  725.6 8.1 collective-permute-start.19
  733.8 8.8 collective-permute-start.20
  750.0 9.9 collective-permute-start.22
  885.7 8.1 collective-permute-start.24
  893.9 8.8 collective-permute-start.25
  904.2 7.5 collective-permute-start.26
  914.6 243.7 %reduce-scatter.18.cloned.1.call-start = ((), (), s32[]{:S(2)}) async-start(), calls=%async_computation.5 | async-start | bytes 184320
  1104.2 8.1 collective-permute-start.28
  1112.4 8.8 collective-permute-start.29
  (30 other events, 536.1 us)
Sparse Core Ops, SparseCore 0:
  63.6 79.0 all-reduce.6
  424.3 35.5 reduce-scatter.13
  603.2 34.3 reduce-scatter.15
  914.7 73.7 all-reduce.8
  1123.5 34.8 reduce-scatter.17
where the time goes:
time: 1180 us; the launch traced here: 1170 us
  blocking collectives  575 us (49%)
  waiting for transfers between devices  385 us (33%)
  starting transfers between devices  87.2 us (7%)
  local copies, waits for them, and re-layouts  65.3 us (6%)
  other arithmetic  21.4 us (2%)
  matrix products  16.6 us (1%)
  between operations  16.1 us (1%)
    all_gather x6, blocking collectives, level_gather(): return lax.all_gather(section, 'leaf', axis=2, tiled=True)  350 us
    unnamed x10, waiting for transfers between devices  258 us
    all_gather x7, blocking collectives, full_columns(): return lax.all_gather(section, 'panel', axis=1, tiled=True)  168 us
    ppermute x30, waiting for transfers between devices, partner(): return lax.ppermute(value, axis, pairs)  128 us
    ppermute x30, starting transfers between devices, partner(): return lax.ppermute(value, axis, pairs)  87 us
    unnamed x2, blocking collectives  57.4 us
  transfers between devices with their start and end apart: 35, of which 35 were waited for; matrix products, arithmetic and copies ran while one was open for 1% of the time, Pallas kernels for 0%

commit v1 on v0

v1 whole, which is shorter than its diff:
```python
import functools

import jax
import jax.numpy as jnp
from jax import lax
from jax.experimental import pallas as pl
from jax.experimental.pallas import tpu as pltpu
from jax.sharding import Mesh
from jax.sharding import PartitionSpec as P

BLOCK = 128
P_SIZE = 5120
U = 2560
PANELS = 8
SHARES = 8
PIVOT_BLOCKS = P_SIZE // BLOCK
UPDATE_BLOCKS = U // BLOCK
ROWS = P_SIZE // PANELS
WIDE = 128

LEAF = ("z2", "z1", "z0", "x", "c")
SHARE = ("x", "c")
DEPTH = ("z2", "z1", "z0")


def exchange(value, axes):
    return lax.all_to_all(value, axes, 0, 0, tiled=True)


def scatter_sum(value, axes):
    return jnp.sum(exchange(value.astype(jnp.bfloat16), axes).astype(jnp.float32), 0)


def gather(value, axes, count):
    return exchange(jnp.broadcast_to(value[None], (count,) + value.shape), axes)


def partner(value):
    return lax.ppermute(value, "z0", [(0, 1), (1, 0)])


def halves(vector):
    half = vector.shape[0] // 2
    other = jnp.concatenate([vector[half:], -vector[:half]], 0)
    return vector.astype(jnp.bfloat16), other.astype(jnp.bfloat16)


def multiply(pieces, matrix_ref, start, span, contract):
    dims = (((1,), (contract,)), ((), ()))
    total = None
    for part, piece in enumerate(pieces):
        matrix = matrix_ref[start : start + span, part].reshape(ROWS, ROWS)
        term = lax.dot_general(piece, matrix, dims, preferred_element_type=jnp.float32)
        total = term if total is None else total + term
    return total


def bring(pack_ref, matrix_ref, sems, rows, offset):
    copies = []
    for share in range(SHARES):
        copies.append(
            pltpu.make_async_copy(
                pack_ref.at[share, :, pl.ds(offset * rows, rows)],
                matrix_ref.at[share],
                sems.at[share],
            )
        )
    for copy in copies:
        copy.start()
    return copies


def take_block(index_ref, held_ref, place):
    per = held_ref.shape[2] // BLOCK
    total = None
    for term in range(index_ref.shape[0]):
        spot = index_ref[term, place]
        safe = jnp.maximum(spot, 0)
        start = pl.multiple_of((safe % per) * BLOCK, BLOCK)
        block = held_ref[safe // per, :, pl.ds(start, BLOCK)].astype(jnp.float32)
        block = jnp.where(spot >= 0, block, 0.0)
        total = block if total is None else total + block
    return total


def params():
    return pltpu.CompilerParams(vmem_limit_bytes=24 * 2**20)


def smem():
    return pl.BlockSpec(memory_space=pltpu.SMEM)


def vmem():
    return pl.BlockSpec(memory_space=pltpu.VMEM)


def hbm():
    return pl.BlockSpec(memory_space=pltpu.HBM)


def in_hbm(value):
    return pltpu.with_memory_space_constraint(value, pltpu.HBM)


def matrix_scratch(rows):
    return [
        pltpu.VMEM((SHARES, 2, rows, ROWS), jnp.bfloat16),
        pltpu.SemaphoreType.DMA((SHARES,)),
    ]


def columns_kernel(rows, offset, updates, has_held, has_base, keep, *refs):
    refs = list(refs)
    index_ref = refs.pop(0) if has_held else None
    live_ref = refs.pop(0) if has_base and has_held else None
    held_ref = refs.pop(0) if has_held else None
    base_ref = refs.pop(0) if has_base else None
    pack_ref = refs.pop(0)
    out_ref = refs.pop(0)
    passed_ref = refs.pop(0) if updates else None
    keep_ref = refs.pop(0) if keep else None
    matrix_ref, sems = refs
    copies = bring(pack_ref, matrix_ref, sems, rows, offset)
    steps = SHARES * rows // ROWS
    span = ROWS // BLOCK
    group = ROWS // rows
    total = None
    for step in range(steps):
        if has_held:
            blocks = []
            for place in range(step * span, (step + 1) * span):
                block = take_block(index_ref, held_ref, place)
                if has_base:
                    base = base_ref[:, place * BLOCK : (place + 1) * BLOCK].astype(jnp.float32)
                    block = jnp.where(place < live_ref[0], base - block, 0.0)
                blocks.append(block)
            vector = jnp.concatenate(blocks, 1)
        else:
            vector = base_ref[:, step * ROWS : (step + 1) * ROWS].astype(jnp.float32)
        if keep:
            keep_ref[:, step * ROWS : (step + 1) * ROWS] = vector.astype(jnp.bfloat16)
        for share in range(step * group, (step + 1) * group):
            copies[share].wait()
        term = multiply(halves(vector), matrix_ref, step * group, group, 0)
        total = term if total is None else total + term
    for place in range(updates):
        passed_ref[:, place * BLOCK : (place + 1) * BLOCK] = take_block(
            index_ref, held_ref, steps * span + place
        )
    result = total.astype(out_ref.dtype)
    for copy in range(out_ref.shape[0]):
        out_ref[copy] = result


def over_columns(
    pack, rows, offset, copies, index=None, held=None, live=None, base=None,
    keep=False, dtype=jnp.bfloat16,
):
    steps = SHARES * rows // ROWS
    updates = index.shape[1] - steps * (ROWS // BLOCK) if index is not None else 0
    args, specs = [], []
    if held is not None:
        args.append(index)
        specs.append(smem())
        if base is not None:
            args.append(live)
            specs.append(smem())
        args.append(held)
        specs.append(vmem())
    if base is not None:
        args.append(base)
        specs.append(vmem())
    args.append(in_hbm(pack))
    specs.append(hbm())
    shapes = [jax.ShapeDtypeStruct((copies, 16, ROWS), dtype)]
    if updates:
        shapes.append(jax.ShapeDtypeStruct((16, updates * BLOCK), jnp.float32))
    if keep:
        shapes.append(jax.ShapeDtypeStruct((16, steps * ROWS), jnp.bfloat16))
    return pl.pallas_call(
        functools.partial(
            columns_kernel, rows, offset, updates, held is not None, base is not None, keep
        ),
        out_shape=shapes,
        in_specs=specs,
        out_specs=[vmem()] * len(shapes),
        scratch_shapes=matrix_scratch(rows),
        compiler_params=params(),
    )(*args)


def rows_kernel(rows, offset, parts, masked, *refs):
    refs = list(refs)
    live_ref = refs.pop(0) if masked else None
    part_refs = [refs.pop(0) for _ in range(parts)]
    held_ref = None if masked else refs.pop(0)
    pack_ref = refs.pop(0)
    out_ref = refs.pop(0)
    keep_ref = refs.pop(0) if masked else None
    matrix_ref, sems = refs
    copies = bring(pack_ref, matrix_ref, sems, rows, offset)
    total = None
    for part_ref in part_refs:
        for copy in range(part_ref.shape[0]):
            term = part_ref[copy].astype(jnp.float32)
            total = term if total is None else total + term
    if masked:
        place = lax.broadcasted_iota(jnp.int32, total.shape, 1) // BLOCK
        total = jnp.where(place < live_ref[0], total, 0.0)
        keep_ref[...] = total.astype(jnp.bfloat16)
    else:
        total = held_ref[...].astype(jnp.float32) - total
    pieces = halves(total)
    group = ROWS // rows
    for step in range(SHARES // group):
        for share in range(step * group, (step + 1) * group):
            copies[share].wait()
        result = multiply(pieces, matrix_ref, step * group, group, 1).astype(jnp.bfloat16)
        for copy in range(out_ref.shape[0]):
            out_ref[copy, :, step * ROWS : (step + 1) * ROWS] = result


def over_rows(pack, rows, offset, copies, parts, live=None, held=None):
    masked = live is not None
    args = ([live] if masked else []) + list(parts) + ([] if masked else [held]) + [in_hbm(pack)]
    specs = ([smem()] if masked else []) + [vmem()] * len(parts)
    specs += ([] if masked else [vmem()]) + [hbm()]
    shapes = [jax.ShapeDtypeStruct((copies, 16, SHARES * rows), jnp.bfloat16)]
    if masked:
        shapes.append(jax.ShapeDtypeStruct((16, ROWS), jnp.bfloat16))
    return pl.pallas_call(
        functools.partial(rows_kernel, rows, offset, len(parts), masked),
        out_shape=shapes,
        in_specs=specs,
        out_specs=[vmem()] * len(shapes),
        scratch_shapes=matrix_scratch(rows),
        compiler_params=params(),
    )(*args)


def crossed(vector):
    row = lax.broadcasted_iota(jnp.int32, (64, 64), 0)
    column = lax.broadcasted_iota(jnp.int32, (64, 64), 1)
    up = (column == row + 1) & (row % 2 == 0)
    down = (column == row - 1) & (row % 2 == 1)
    turn = jnp.where(up, 1.0, jnp.where(down, -1.0, 0.0)).astype(jnp.bfloat16)
    return jnp.dot(turn, vector, preferred_element_type=jnp.float32).astype(jnp.bfloat16)


def pair_dot(vector, other, matrix):
    dims = (((1,), (1,)), ((), ()))
    one = lax.dot_general(vector, matrix[0], dims, preferred_element_type=jnp.float32)
    return one + lax.dot_general(other, matrix[1], dims, preferred_element_type=jnp.float32)


def fetch(own_ref, matrix_ref, sem):
    copy = pltpu.make_async_copy(own_ref, matrix_ref, sem)
    copy.start()
    return copy


def lower_pivots_kernel(
    info_ref, every_ref, own_ref, other_ref, out_ref, matrix_ref, sem
):
    fetched = fetch(own_ref, matrix_ref, sem)
    place = lax.broadcasted_iota(jnp.int32, (64, ROWS), 1) // BLOCK
    sides = []
    for side in range(2):
        value = every_ref[side * 64 : (side + 1) * 64, :ROWS].astype(jnp.float32)
        sides.append(jnp.where(place + side * (ROWS // BLOCK) < info_ref[0], value, 0.0))
    even = info_ref[1] == 0
    vectors = (jnp.where(even, sides[0], sides[1]), jnp.where(even, sides[1], sides[0]))
    row = lax.broadcasted_iota(jnp.int32, (128, 128), 0)
    source = (row % 2) * 64 + (row // 2 % 8) * 8 + (row // 32) * 2 + row // 16 % 2
    order = (lax.broadcasted_iota(jnp.int32, (128, 128), 1) == source).astype(jnp.bfloat16)
    extra = jnp.dot(order, every_ref[:, ROWS:], preferred_element_type=jnp.float32)
    extra = extra.astype(jnp.bfloat16)
    total = None
    for side in (1, 0):
        vector = vectors[side].astype(jnp.bfloat16)
        if side == 0:
            fetched.wait()
        term = pair_dot(vector, crossed(vector), (matrix_ref, other_ref)[side])
        total = term if total is None else total + term
    total = total.astype(jnp.bfloat16)
    for copy in range(4):
        out_ref[copy, :64] = total
        out_ref[copy, 64:] = extra[copy * 32 : (copy + 1) * 32]


def lower_pivots(info, every, own, other):
    return pl.pallas_call(
        lower_pivots_kernel,
        out_shape=jax.ShapeDtypeStruct((4, 96, ROWS), jnp.bfloat16),
        in_specs=[smem(), vmem(), hbm(), vmem()],
        out_specs=vmem(),
        scratch_shapes=[
            pltpu.VMEM(own.shape, jnp.bfloat16),
            pltpu.SemaphoreType.DMA,
        ],
        compiler_params=params(),
    )(info, every, in_hbm(own), other)


def lower_updates_kernel(
    info_ref, got_ref, own_ref, other_ref, out_ref, solved_ref, matrix_ref, sem
):
    fetched = fetch(own_ref, matrix_ref, sem)
    total = None
    for copy in range(4):
        term = got_ref[copy, :64].astype(jnp.float32)
        total = term if total is None else total + term
    place = lax.broadcasted_iota(jnp.int32, (64, ROWS), 1) // BLOCK
    vector = jnp.where(place < info_ref[0], total, 0.0).astype(jnp.bfloat16)
    solved_ref[...] = vector
    row = lax.broadcasted_iota(jnp.int32, (64, 64), 0)
    source = (row // 2 % 8) * 8 + (row // 16) * 2 + row % 2
    order = (lax.broadcasted_iota(jnp.int32, (64, 64), 1) == source).astype(jnp.bfloat16)
    vector = jnp.dot(order, vector, preferred_element_type=jnp.float32).astype(jnp.bfloat16)
    turn = crossed(vector)
    other = pair_dot(vector, turn, other_ref)
    fetched.wait()
    sides = [pair_dot(vector, turn, matrix_ref), other]
    even = info_ref[1] == 0
    own = sides[0].shape[1]
    first = jnp.where(even, sides[0], sides[1]).astype(jnp.bfloat16)
    second = jnp.where(even, sides[1], sides[0]).astype(jnp.bfloat16)
    for copy in range(2):
        out_ref[copy, :, :own] = first
        out_ref[copy, :, own:] = second


def lower_updates(info, got, own, other):
    return pl.pallas_call(
        lower_updates_kernel,
        out_shape=[
            jax.ShapeDtypeStruct((2, 64, ROWS), jnp.bfloat16),
            jax.ShapeDtypeStruct((64, ROWS), jnp.bfloat16),
        ],
        in_specs=[smem(), vmem(), hbm(), vmem()],
        out_specs=[vmem()] * 2,
        scratch_shapes=[
            pltpu.VMEM(own.shape, jnp.bfloat16),
            pltpu.SemaphoreType.DMA,
        ],
        compiler_params=params(),
    )(info, got, in_hbm(own), other)


def hand_kernel(masked, added, tailed, *refs):
    refs = list(refs)
    live_ref = refs.pop(0) if masked else None
    part_ref = refs.pop(0)
    more_ref = refs.pop(0) if added else None
    tail_ref = refs.pop(0) if tailed else None
    out_ref = refs.pop(0)
    total = part_ref[0].astype(jnp.float32)
    for copy in range(1, part_ref.shape[0]):
        total = total + part_ref[copy].astype(jnp.float32)
    if added:
        total = total + more_ref[...]
    if masked:
        place = lax.broadcasted_iota(jnp.int32, total.shape, 1) // BLOCK
        total = jnp.where(place < live_ref[0], total, 0.0)
    total = total.astype(jnp.bfloat16)
    for copy in range(out_ref.shape[0]):
        out_ref[copy, :, : total.shape[1]] = total
        if tailed:
            out_ref[copy, :, total.shape[1] :] = tail_ref[...]


def hand_on(part, copies, live=None, more=None, tail=None):
    width = part.shape[2] + (tail.shape[1] if tail is not None else 0)
    args = [item for item in (live, part, more, tail) if item is not None]
    specs = [smem()] * (live is not None) + [vmem()] * (len(args) - (live is not None))
    return pl.pallas_call(
        functools.partial(hand_kernel, live is not None, more is not None, tail is not None),
        out_shape=jax.ShapeDtypeStruct((copies, 16, width), jnp.bfloat16),
        in_specs=specs,
        out_specs=vmem(),
        compiler_params=params(),
    )(*args)


def pick_kernel(index_ref, held_ref, out_ref):
    for place in range(index_ref.shape[1]):
        out_ref[:, place * BLOCK : (place + 1) * BLOCK] = take_block(index_ref, held_ref, place)


def take_blocks(index, held):
    return pl.pallas_call(
        pick_kernel,
        out_shape=jax.ShapeDtypeStruct((held.shape[1], index.shape[1] * BLOCK), jnp.float32),
        in_specs=[smem(), pl.BlockSpec(memory_space=pltpu.VMEM)],
        out_specs=pl.BlockSpec(memory_space=pltpu.VMEM),
        compiler_params=params(),
    )(index, held)


def last_kernel(got_ref, own_ref, out_ref, matrix_ref, sem):
    fetched = fetch(own_ref, matrix_ref, sem)
    stacked = jnp.concatenate([got_ref[share, :16] for share in range(SHARES)], 0)
    row = lax.broadcasted_iota(jnp.int32, (WIDE, WIDE), 0)
    column = lax.broadcasted_iota(jnp.int32, (WIDE, WIDE), 1)
    total = None
    for part in range(2):
        imaginary = (row // 8 + part) % 2
        source = row % 8 * 16 + imaginary * 8 + row // 16
        sign = jnp.where((row // 8 % 2 == 1) & (part == 1), -1.0, 1.0)
        order = jnp.where(column == source, sign, 0.0).astype(jnp.bfloat16)
        vector = jnp.dot(order, stacked, preferred_element_type=jnp.float32)
        if part == 0:
            fetched.wait()
        term = jnp.dot(
            vector.astype(jnp.bfloat16), matrix_ref[part], preferred_element_type=jnp.float32
        )
        total = term if total is None else total + term
    out_ref[...] = total.astype(jnp.bfloat16)


def last_product(got, own):
    return pl.pallas_call(
        last_kernel,
        out_shape=jax.ShapeDtypeStruct((WIDE, ROWS), jnp.bfloat16),
        in_specs=[vmem(), hbm()],
        out_specs=vmem(),
        scratch_shapes=[pltpu.VMEM(own.shape, jnp.bfloat16), pltpu.SemaphoreType.DMA],
        compiler_params=params(),
    )(got, in_hbm(own))


def shards(
    inverse_root,
    inverse_upper,
    inverse_middle,
    inverse_lower,
    coupling_upper,
    coupling_middle,
    coupling_lower,
    source_root,
    source_upper,
    source_middle,
    source_lower,
    blocks_upper,
    blocks_middle,
    blocks_lower,
    live_blocks,
):
    tables = (None, blocks_upper, blocks_middle, blocks_lower)
    sources = (source_root, source_upper, source_middle, source_lower)
    depth = lax.axis_index(DEPTH)
    share = lax.axis_index(SHARE)
    column = lax.axis_index("panel")

    packs = [
        jnp.concatenate([inverse_middle.swapaxes(1, 2), coupling_middle], 1),
        jnp.concatenate(
            [inverse_upper.swapaxes(1, 2), coupling_upper, inverse_root.swapaxes(1, 2)], 1
        ),
        coupling_lower,
    ]
    packs = [lax.all_gather(pack, SHARE, axis=0, tiled=False) for pack in packs]
    pivot_at = {2: (packs[0], 320, 0), 1: (packs[1], 160, 0), 0: (packs[1], 80, 3)}
    update_at = {2: (packs[0], 160, 2), 1: (packs[1], 80, 2)}

    def front_of(level):
        width = 8 >> level
        return depth // width, depth % width

    def live_of(level):
        front, _ = front_of(level)
        return lax.dynamic_slice_in_dim(live_blocks, (1 << level) - 1 + front, 1, 0)[0]

    def panel_live(level):
        return (live_of(level) - column * (ROWS // BLOCK))[None]

    def depth_live(level):
        return (live_of(level) - front_of(level)[1] * (PIVOT_BLOCKS // (8 >> level)))[None]

    def incoming(level):
        front, within = front_of(level)
        pair = lax.dynamic_slice_in_dim(tables[level + 1], 2 * front, 2, 0)
        pivots = PIVOT_BLOCKS // (8 >> level)
        goal = within * pivots + jnp.arange(pivots, dtype=jnp.int32)
        if level >= 1:
            updates = UPDATE_BLOCKS // (8 >> level)
            extra = PIVOT_BLOCKS + within * updates + jnp.arange(updates, dtype=jnp.int32)
            goal = jnp.concatenate([goal, extra])
        order = jnp.arange(2 * UPDATE_BLOCKS, dtype=jnp.int32).reshape(2, 1, UPDATE_BLOCKS)
        match = pair[:, None, :] == goal[None, :, None]
        return jnp.max(jnp.where(match, order, -1), 2)

    def picking(level, complete=False):
        front, within = front_of(level)
        parts = 16 >> level
        pivots = PIVOT_BLOCKS // parts
        updates = UPDATE_BLOCKS // parts if level >= 2 else 0
        own = UPDATE_BLOCKS // (8 >> level)
        row = lax.dynamic_slice_in_dim(tables[level], front, 1, 0)[0]
        if not complete:
            row = lax.dynamic_slice_in_dim(row, within * own, own, 0)
        whole = pivots + updates
        spot = row // pivots * whole + row % pivots
        if updates:
            rest = row - PIVOT_BLOCKS
            spot = jnp.where(rest >= 0, rest // updates * whole + pivots + rest % updates, spot)
        return spot[None]

    def handing():
        row = lax.dynamic_slice_in_dim(tables[3], depth, 1, 0)
        pivots = PIVOT_BLOCKS // 2
        updates = UPDATE_BLOCKS // 2
        rest = row - PIVOT_BLOCKS
        later = rest // updates * (pivots + updates) + pivots + rest % updates
        return jnp.where(rest >= 0, later, row // pivots * (pivots + updates) + row % pivots)

    core = lax.axis_index("c")
    other_inverse = lax.ppermute(inverse_lower, "c", [(0, 1), (1, 0)])
    other_coupling = lax.ppermute(coupling_lower, "c", [(0, 1), (1, 0)])
    packed = [source_lower] + [sources[level] for level in (2, 1, 0)]
    widths = [piece.shape[2] for piece in packed[1:]]
    packed = jnp.concatenate(packed, 2)
    packed = jnp.pad(packed, ((0, 0), (0, 0), (0, 2 * ROWS - packed.shape[2])))
    packed = packed.reshape(2, 4, 2, 2 * ROWS).transpose(2, 1, 0, 3).reshape(2, 1, 8, 2 * ROWS)
    packed = jnp.broadcast_to(packed, (2, PANELS, 8, 2 * ROWS)).reshape(16, 8, 2 * ROWS)
    every = exchange(packed, ("c", "panel")).reshape(WIDE, 2 * ROWS)
    place = lax.axis_index("x") * 2
    span = ROWS // BLOCK
    info = jnp.stack([live_of(3) - place * span, core])
    partial = lower_pivots(info, every, inverse_lower, other_inverse)
    got = exchange(partial, "x")
    info = jnp.stack([live_of(3) - column * span, core])
    update, solved = lower_updates(info, got, coupling_lower, other_coupling)
    solved_mine = lax.dynamic_slice_in_dim(
        solved.reshape(PANELS, 4, 2, ROWS), lax.axis_index("x"), 1, 1
    )
    solved_mine = solved_mine[:, 0].transpose(1, 0, 2).reshape(16, ROWS)

    children = exchange(update.reshape(64, 2, ROWS), ("z0", "x", "panel"))
    children = children.reshape(8, PANELS, 2, ROWS).astype(jnp.float32)
    children = jnp.sum(children, 1).astype(jnp.bfloat16)
    children = children.transpose(1, 0, 2).reshape(2, P_SIZE)
    spread = gather(children, "panel", PANELS).transpose(1, 0, 2).reshape(16, P_SIZE)
    gathered = spread[None]
    base = {}
    start = 0
    extra = got[:, 64:].reshape(4, 16, 2, ROWS).transpose(1, 0, 2, 3)
    for level, width in zip((2, 1, 0), widths):
        base[level] = extra[:, :, :, start : start + width].reshape(16, SHARES * width)
        start += width

    held = {}
    for level in (2, 1, 0):
        count = 8 >> level
        found = over_columns(
            *pivot_at[level],
            1 if level == 2 else count,
            index=incoming(level),
            held=gathered,
            live=depth_live(level),
            base=base[level],
        )
        if level == 2:
            parts = [found[0], partner(found[0])]
        else:
            parts = [exchange(found[0], DEPTH[level:])]
        if level >= 1:
            update, held[level] = over_rows(
                *update_at[level], PANELS, parts, live=panel_live(level)
            )
            update = hand_on(exchange(update, "panel"), 2 * count, more=found[1])
            gathered = exchange(update, DEPTH[level - 1 :])

    answers = []
    picked = None
    for level in (0, 1, 2):
        count = 8 >> level
        if level == 0:
            answer, _ = over_rows(*pivot_at[0], PANELS, parts, live=panel_live(0))
        else:
            partial, picked = over_columns(
                *update_at[level],
                1 if level == 2 else count,
                index=picking(level),
                held=gathered,
                keep=True,
            )
            if level == 2:
                parts = [partial, partner(partial)]
            else:
                parts = [exchange(partial, DEPTH[level:])]
            (answer,) = over_rows(
                *pivot_at[level], 1 if level == 2 else PANELS, parts, held=held[level]
            )
        if level < 2:
            outgoing = hand_on(
                exchange(answer, "panel"), count, live=depth_live(level), tail=picked
            )
            mine = outgoing[0, :, : P_SIZE // count].reshape(2, PANELS, -1)
            answers.append(lax.dynamic_slice_in_dim(mine, column, 1, 1)[:, 0])
            gathered = exchange(outgoing, DEPTH[level:])
        else:
            answer = answer.reshape(2, PANELS, -1).transpose(1, 0, 2)
            answer = exchange(jnp.concatenate([answer, answer], 0), ("z0", "panel"))
            answer = answer.reshape(2, PANELS, 2, -1).astype(jnp.float32)
            row_mask = (jnp.arange(P_SIZE, dtype=jnp.int32) // BLOCK < live_of(2)).reshape(2, 1, -1)
            both = (jnp.sum(answer, 1) * row_mask).astype(jnp.bfloat16)
            answers.append(lax.dynamic_slice_in_dim(both, front_of(2)[1], 1, 0)[0])

    passed = take_blocks(picking(2, True), gathered).reshape(2, PANELS, 2, -1)
    passed = lax.dynamic_slice_in_dim(passed, column, 1, 1)[:, 0].transpose(1, 0, 2)
    both = jnp.concatenate([both.astype(jnp.float32), passed], 2)
    handed = take_blocks(handing(), both).astype(jnp.bfloat16)
    vector = gather(handed, "panel", PANELS).transpose(1, 0, 2).reshape(16, U)
    (partial,) = over_columns(packs[2], 320, 0, 1, base=vector, dtype=jnp.float32)
    target = (solved_mine.astype(jnp.float32) - partial[0]).astype(jnp.bfloat16)
    smaller = [answer.reshape(2, SHARES, -1).transpose(1, 0, 2) for answer in answers]
    counts = [piece.shape[2] for piece in smaller]
    smaller = jnp.concatenate(smaller, 2)
    smaller = jnp.pad(smaller, ((0, 0), (0, 0), (0, ROWS - smaller.shape[2])))
    target = jnp.broadcast_to(target[None], (SHARES, 16, ROWS))
    got = exchange(jnp.concatenate([target, smaller], 1), SHARE)
    last = last_product(got, inverse_lower)
    lower_rows = share * ROWS + jnp.arange(ROWS, dtype=jnp.int32)
    lower_mask = (lower_rows // BLOCK < live_of(3)).astype(jnp.float32)[None, :]
    lower = scatter_sum(last.reshape(PANELS, 16, ROWS), "panel") * lower_mask

    got = got[:, 16:].transpose(1, 0, 2).astype(jnp.float32)
    outs = []
    start = 0
    for width in counts:
        outs.append(got[:, :, start : start + width])
        start += width
    return (outs[0], outs[1], outs[2], lower.reshape(2, SHARES, ROWS))


def solution(mesh):
    split = Mesh(mesh.devices.reshape(2, 2, 2, 4, 2, PANELS), LEAF + ("panel",))
    by_rows = P(None, "panel", LEAF)
    by_updates = P(None, LEAF, "panel")
    return jax.shard_map(
        shards,
        mesh=split,
        in_specs=(by_rows,) * 4 + (by_updates,) * 3 + (by_rows,) * 4 + (P(),) * 4,
        out_specs=(by_rows,) * 4,
        check_vma=False,
    )
```

time: 1180 us -> 344 us (0.29)
  blocking collectives: 575 us -> 35.9 us
  waiting for transfers between devices: 385 us -> 133 us
  local copies, waits for them, and re-layouts: 65.3 us -> 9.8 us
  Pallas kernels: 0 us -> 49.2 us
  matrix products: 16.6 us -> 0 us
    all_gather x13 -> x0, blocking collectives: 517 us -> none  [the longest x6 350 us: level_gather(): return lax.all_gather(section, 'leaf', axis=2, tiled=True)]
    unnamed x10 -> x3, waiting for transfers between devices: 258 us -> 0.71 us
    all_to_all x0 -> x16, waiting for transfers between devices: none -> 126 us  [exchange(): return lax.all_to_all(value, axes, 0, 0, tiled=True)]
    ppermute x30 -> x4, waiting for transfers between devices: 128 us -> 4.19 us  [the longest x2 4.18 us: partner(): return lax.ppermute(value, 'z0', [(0, 1), (1, 0)])]
    ppermute x30 -> x4, starting transfers between devices: 87 us -> 9.87 us  [the longest x2 5.64 us: partner(): return lax.ppermute(value, 'z0', [(0, 1), (1, 0)])]
    all_to_all x0 -> x16, starting transfers between devices: none -> 72.9 us  [exchange(): return lax.all_to_all(value, axes, 0, 0, tiled=True)]
    unnamed x2 -> x0, blocking collectives: 57.4 us -> none
    pallas_call x0 -> x20, Pallas kernels: none -> 49.2 us  [the longest x6 19.2 us: over_columns(): pl.pallas_call(functools.partial(columns_kernel, rows, offset, updates, h...]
  transfers between devices with their start and end apart: 35 -> 23, of which waited for: 35 -> 19; matrix products, arithmetic and copies ran while one was open for 1% -> 5% of each run, Pallas kernels for 0% -> 13%
where the time goes in v1:
time: 344 us; the launch traced here: 341 us
  waiting for transfers between devices  133 us (39%)
  starting transfers between devices  82.9 us (24%)
  Pallas kernels  49.2 us (14%)
  blocking collectives  35.9 us (10%)
  between operations  19.8 us (6%)
  local copies, waits for them, and re-layouts  9.8 us (3%)
  other arithmetic  9.7 us (3%)
    all_to_all x16, waiting for transfers between devices, exchange(): return lax.all_to_all(value, axes, 0, 0, tiled=True)  126 us
    all_to_all x16, starting transfers between devices, exchange(): return lax.all_to_all(value, axes, 0, 0, tiled=True)  72.9 us
    all_to_all x3, blocking collectives, exchange(): return lax.all_to_all(value, axes, 0, 0, tiled=True)  35.9 us
    pallas_call x6, Pallas kernels, over_columns(): pl.pallas_call(functools.partial(columns_kernel, rows, offset, updates, h...  19.2 us
    pallas_call x5, Pallas kernels, over_rows(): pl.pallas_call(functools.partial(rows_kernel, rows, offset, len(parts), m...  16.6 us
  transfers between devices with their start and end apart: 23, of which 19 were waited for; matrix products, arithmetic and copies ran while one was open for 5% of the time, Pallas kernels for 13%

profile of v1, /device:TPU:6, one launch (start us, length us, event | category | flops | bytes accessed | tf_op | source)
XLA Modules:
  0.0 340.6 jit_solution(9630395170994824532)
XLA Ops:
  14.6 7.3 %all-to-all-start = ((bf16[16,8,1280]{2,1,0:T(8,128)(2,1)}), bf16[16,8,1280]{2,1,0:T(8,128)(2,1)S(1)}, u32[]{:S(2)}, u32[]{:S(2)}) async-start(bf16[16,8,1280]{2,1,0:T(8,128)(2,1)} %bitcast.6), calls=%async_computation | async-start | bytes 655360 | tf_op jit(solution)/shard_map/all_to_all | solution.py:27
  25.7 8.1 %all-to-all-done = bf16[16,8,1280]{2,1,0:T(8,128)(2,1)S(1)} async-done(((bf16[16,8,1280]{2,1,0:T(8,128)(2,1)}), bf16[16,8,1280]{2,1,0:T(8,128)(2,1)S(1)}, u32[]{:S(2)}, u32[]{:S(2)}) %all-to-all-start) | async-done | bytes 327712 | tf_op jit(solution)/shard_map/all_to_all | solution.py:27
  38.0 5.5 %all-to-all-start.1 = ((bf16[4,96,640]{2,1,0:T(8,128)(2,1)}), bf16[4,96,640]{2,1,0:T(8,128)(2,1)S(1)}, u32[]{:S(2)}, u32[]{:S(2)}) async-start(bf16[4,96,640]{2,1,0:T(8,128)(2,1)} %shard_map.174), calls=%async_computation.1 | async-start | bytes 983040 | tf_op jit(solution)/shard_map/all_to_all | solution.py:27
  44.2 12.4 %all-to-all-done.1.got_ref = bf16[4,96,640]{2,1,0:T(8,128)(2,1)S(1)} async-done(((bf16[4,96,640]{2,1,0:T(8,128)(2,1)}), bf16[4,96,640]{2,1,0:T(8,128)(2,1)S(1)}, u32[]{:S(2)}, u32[]{:S(2)}) %all-to-all-start.1) | async-done | bytes 491552 | tf_op jit(solution)/shard_map/all_to_all | solution.py:27
  59.5 8.6 %all-to-all-start.2 = ((bf16[64,2,640]{2,1,0:T(2,128)(2,1)}), bf16[64,2,640]{2,1,0:T(2,128)(2,1)S(1)}, u32[]{:S(2)}, u32[]{:S(2)}) async-start(bf16[64,2,640]{2,1,0:T(2,128)(2,1)} %reshape.188), calls=%async_computation.2 | async-start | bytes 327680 | tf_op jit(solution)/shard_map/all_to_all | solution.py:27
  68.9 9.6 %all-to-all-done.2 = bf16[64,2,640]{2,1,0:T(2,128)(2,1)S(1)} async-done(((bf16[64,2,640]{2,1,0:T(2,128)(2,1)}), bf16[64,2,640]{2,1,0:T(2,128)(2,1)S(1)}, u32[]{:S(2)}, u32[]{:S(2)}) %all-to-all-start.2) | async-done | bytes 163872 | tf_op jit(solution)/shard_map/all_to_all | solution.py:27
  84.2 8.0 %all-to-all-done.3 = bf16[8,2,5120]{2,1,0:T(2,128)(2,1)S(1)} async-done(((bf16[8,2,5120]{2,1,0:T(2,128)(2,1)}), bf16[8,2,5120]{2,1,0:T(2,128)(2,1)S(1)}, u32[]{:S(2)}, u32[]{:S(2)}) %all-to-all-start.3) | async-done | bytes 163872 | tf_op jit(solution)/shard_map/all_to_all | solution.py:27
  109.2 11.1 %all-to-all-done.4.refs_0_ = bf16[8,16,1280]{2,1,0:T(8,128)(2,1)S(1)} async-done(((bf16[8,16,1280]{2,1,0:T(8,128)(2,1)}), bf16[8,16,1280]{2,1,0:T(8,128)(2,1)S(1)}, u32[]{:S(2)}, u32[]{:S(2)}) %all-to-all-start.4) | async-done | bytes 327712 | tf_op jit(solution)/shard_map/all_to_all | solution.py:27
  121.0 5.4 %all-to-all-start.5 = ((bf16[4,16,1280]{2,1,0:T(8,128)(2,1)}), bf16[4,16,1280]{2,1,0:T(8,128)(2,1)S(1)}, u32[]{:S(2)}, u32[]{:S(2)}) async-start(bf16[4,16,1280]{2,1,0:T(8,128)(2,1)} %shard_map.178), calls=%async_computation.5 | async-start | bytes 327680 | tf_op jit(solution)/shard_map/all_to_all | solution.py:27
  140.1 5.1 %all-to-all-done.6.refs_1_ = bf16[4,16,640]{2,1,0:T(8,128)(2,1)S(1)} async-done(((bf16[4,16,640]{2,1,0:T(8,128)(2,1)}), bf16[4,16,640]{2,1,0:T(8,128)(2,1)S(1)}, u32[]{:S(2)}, u32[]{:S(2)}) %all-to-all-start.6) | async-done | bytes 81952 | tf_op jit(solution)/shard_map/all_to_all | solution.py:27
  147.4 15.9 %all_to_all.95.refs_0_ = bf16[8,16,640]{2,1,0:T(8,128)(2,1)S(1)} all-to-all(bf16[8,16,640]{2,1,0:T(8,128)(2,1)S(1)} %get-tuple-element.24), channel_id=1, replica_groups=mesh['z2'=2,'z1'=2,'z0'=2,'x'=4,'c'=2,'panel'=8] {'panel'}, dimensions={0} | all-to-all | bytes 327680 | tf_op jit(solution)/shard_map/all_to_all | solution.py:27
  164.0 5.6 %all-to-all-start.8 = ((bf16[8,16,640]{2,1,0:T(8,128)(2,1)}), bf16[8,16,640]{2,1,0:T(8,128)(2,1)S(1)}, u32[]{:S(2)}, u32[]{:S(2)}) async-start(bf16[8,16,640]{2,1,0:T(8,128)(2,1)} %shard_map.181), calls=%async_computation.8 | async-start | bytes 327680 | tf_op jit(solution)/shard_map/all_to_all | solution.py:27
  170.8 8.2 %all-to-all-done.8.refs_2_ = bf16[8,16,640]{2,1,0:T(8,128)(2,1)S(1)} async-done(((bf16[8,16,640]{2,1,0:T(8,128)(2,1)}), bf16[8,16,640]{2,1,0:T(8,128)(2,1)S(1)}, u32[]{:S(2)}, u32[]{:S(2)}) %all-to-all-start.8) | async-done | bytes 163872 | tf_op jit(solution)/shard_map/all_to_all | solution.py:27
  186.2 8.7 %all-to-all-done.9.refs_1_ = bf16[8,16,640]{2,1,0:T(8,128)(2,1)S(1)} async-done(((bf16[8,16,640]{2,1,0:T(8,128)(2,1)}), bf16[8,16,640]{2,1,0:T(8,128)(2,1)S(1)}, u32[]{:S(2)}, u32[]{:S(2)}) %all-to-all-start.9) | async-done | bytes 163872 | tf_op jit(solution)/shard_map/all_to_all | solution.py:27
  197.1 11.8 %all_to_all.96.refs_1_ = bf16[8,16,640]{2,1,0:T(8,128)(2,1)S(1)} all-to-all(bf16[8,16,640]{2,1,0:T(8,128)(2,1)S(1)} %get-tuple-element.26), channel_id=1, replica_groups=mesh['z2'=2,'z1'=2,'z0'=2,'x'=4,'c'=2,'panel'=8] {'panel'}, dimensions={0} | all-to-all | bytes 327680 | tf_op jit(solution)/shard_map/all_to_all | solution.py:27
  213.1 9.2 %all-to-all-done.11.refs_1_ = bf16[8,16,640]{2,1,0:T(8,128)(2,1)S(1)} async-done(((bf16[8,16,640]{2,1,0:T(8,128)(2,1)}), bf16[8,16,640]{2,1,0:T(8,128)(2,1)S(1)}, u32[]{:S(2)}, u32[]{:S(2)}) %all-to-all-start.11) | async-done | bytes 163872 | tf_op jit(solution)/shard_map/all_to_all | solution.py:27
  224.8 8.2 %all_to_all.97.refs_0_ = bf16[4,16,640]{2,1,0:T(8,128)(2,1)S(1)} all-to-all(bf16[4,16,640]{2,1,0:T(8,128)(2,1)S(1)} %get-tuple-element.27), channel_id=1, replica_groups=mesh['z2'=2,'z1'=2,'z0'=2,'x'=4,'c'=2,'panel'=8] {'z1','z0'}, dimensions={0} | all-to-all | bytes 163840 | tf_op jit(solution)/shard_map/all_to_all | solution.py:27
  241.0 10.2 %all-to-all-done.13.refs_1_ = bf16[8,16,1280]{2,1,0:T(8,128)(2,1)S(1)} async-done(((bf16[8,16,1280]{2,1,0:T(8,128)(2,1)}), bf16[8,16,1280]{2,1,0:T(8,128)(2,1)S(1)}, u32[]{:S(2)}, u32[]{:S(2)}) %all-to-all-start.13) | async-done | bytes 327712 | tf_op jit(solution)/shard_map/all_to_all | solution.py:27
  256.4 5.6 %all-to-all-done.14.refs_1_.held_ref = bf16[4,16,1920]{2,1,0:T(8,128)(2,1)S(1)} async-done(((bf16[4,16,1920]{2,1,0:T(8,128)(2,1)}), bf16[4,16,1920]{2,1,0:T(8,128)(2,1)S(1)}, u32[]{:S(2)}, u32[]{:S(2)}) %all-to-all-start.14) | async-done | bytes 245792 | tf_op jit(solution)/shard_map/all_to_all | solution.py:27
  281.6 7.2 %all-to-all-done.15 = bf16[16,2,2560]{2,1,0:T(2,128)(2,1)S(1)} async-done(((bf16[16,2,2560]{2,1,0:T(2,128)(2,1)}), bf16[16,2,2560]{2,1,0:T(2,128)(2,1)S(1)}, u32[]{:S(2)}, u32[]{:S(2)}) %all-to-all-start.15) | async-done | bytes 163872 | tf_op jit(solution)/shard_map/all_to_all | solution.py:27
  294.3 8.3 %all-to-all-done.16 = bf16[8,2,2560]{2,1,0:T(2,128)(2,1)S(1)} async-done(((bf16[8,2,2560]{2,1,0:T(2,128)(2,1)}), bf16[8,2,2560]{2,1,0:T(2,128)(2,1)S(1)}, u32[]{:S(2)}, u32[]{:S(2)}) %all-to-all-start.16) | async-done | bytes 81952 | tf_op jit(solution)/shard_map/all_to_all | solution.py:27
  306.7 5.7 %all-to-all-start.17 = ((bf16[8,18,640]{2,1,0:T(8,128)(2,1)}), bf16[8,18,640]{2,1,0:T(8,128)(2,1)S(1)}, u32[]{:S(2)}, u32[]{:S(2)}) async-start(bf16[8,18,640]{2,1,0:T(8,128)(2,1)} %pad_maximum_fusion.2), calls=%async_computation.17 | async-start | bytes 491520 | tf_op jit(solution)/shard_map/all_to_all | solution.py:27
  312.4 5.3 %all-to-all-done.17.got_ref = bf16[8,18,640]{2,1,0:T(8,128)(2,1)S(1)} async-done(((bf16[8,18,640]{2,1,0:T(8,128)(2,1)}), bf16[8,18,640]{2,1,0:T(8,128)(2,1)S(1)}, u32[]{:S(2)}, u32[]{:S(2)}) %all-to-all-start.17) | async-done | bytes 184352 | tf_op jit(solution)/shard_map/all_to_all | solution.py:27
  326.5 6.9 %all-to-all-done.18 = bf16[8,16,640]{2,1,0:T(8,128)(2,1)S(1)} async-done(((bf16[8,16,640]{2,1,0:T(8,128)(2,1)}), bf16[8,16,640]{2,1,0:T(8,128)(2,1)S(1)}, u32[]{:S(2)}, u32[]{:S(2)}) %all-to-all-start.18) | async-done | bytes 163872 | tf_op jit(solution)/shard_map/all_to_all | solution.py:27
  (151 shorter events, 122.9 us)
Async XLA Ops:
  7.2 85.1 %all-gather.7.cloned.1.call-start = ((), (), s32[]{:S(2)}) async-start(), calls=%async_computation.19 | async-start | bytes 11059200 | tf_op jit(solution)/shard_map/all_gather | solution.py:463
  9.8 121.1 %all-gather.9.cloned.1.call-start = ((), (), s32[]{:S(2)}) async-start(), calls=%async_computation.20 | async-start | bytes 7372800 | tf_op jit(solution)/shard_map/all_gather | solution.py:463
  11.0 291.7 %all-gather.11.cloned.1.call-start = ((), (), s32[]{:S(2)}) async-start(), calls=%async_computation.21 | async-start | bytes 7372800 | tf_op jit(solution)/shard_map/all_gather | solution.py:463
  11.7 22.1 %collective-permute-start = (bf16[2,640,640]{2,1,0:T(8,128)(2,1)}, bf16[2,640,640]{2,1,0:T(8,128)(2,1)S(1)}, u32[]{:S(2)}, u32[]{:S(2)}) collective-permute-start(bf16[2,640,640]{2,1,0:T(8,128)(2,1)} %own_ref.5), channel_id=1, source_target_pairs={{0,8},{8,0},{1,9},{9,1},{2,10},{10,2},{3,11},{11,3},{4,12},{12,4},... | collective-permute-start | bytes 4915208 | tf_op jit(solution)/shard_map/ppermute | solution.py:519
  14.6 19.2 %all-to-all-start = ((bf16[16,8,1280]{2,1,0:T(8,128)(2,1)}), bf16[16,8,1280]{2,1,0:T(8,128)(2,1)S(1)}, u32[]{:S(2)}, u32[]{:S(2)}) async-start(bf16[16,8,1280]{2,1,0:T(8,128)(2,1)} %bitcast.6), calls=%async_computation | async-start | bytes 655360 | tf_op jit(solution)/shard_map/all_to_all | solution.py:27
  22.0 22.2 %collective-permute-start.1 = (bf16[2,320,640]{2,1,0:T(8,128)(2,1)}, bf16[2,320,640]{2,1,0:T(8,128)(2,1)S(1)}, u32[]{:S(2)}, u32[]{:S(2)}) collective-permute-start(bf16[2,320,640]{2,1,0:T(8,128)(2,1)} %own_ref.4), channel_id=1, source_target_pairs={{0,8},{8,0},{1,9},{9,1},{2,10},{10,2},{3,11},{11,3},{4,12},{12,4},... | collective-permute-start | bytes 2457608 | tf_op jit(solution)/shard_map/ppermute | solution.py:520
  38.0 18.6 %all-to-all-start.1 = ((bf16[4,96,640]{2,1,0:T(8,128)(2,1)}), bf16[4,96,640]{2,1,0:T(8,128)(2,1)S(1)}, u32[]{:S(2)}, u32[]{:S(2)}) async-start(bf16[4,96,640]{2,1,0:T(8,128)(2,1)} %shard_map.174), calls=%async_computation.1 | async-start | bytes 983040 | tf_op jit(solution)/shard_map/all_to_all | solution.py:27
  59.5 19.0 %all-to-all-start.2 = ((bf16[64,2,640]{2,1,0:T(2,128)(2,1)}), bf16[64,2,640]{2,1,0:T(2,128)(2,1)S(1)}, u32[]{:S(2)}, u32[]{:S(2)}) async-start(bf16[64,2,640]{2,1,0:T(2,128)(2,1)} %reshape.188), calls=%async_computation.2 | async-start | bytes 327680 | tf_op jit(solution)/shard_map/all_to_all | solution.py:27
  79.5 12.7 %all-to-all-start.3 = ((bf16[8,2,5120]{2,1,0:T(2,128)(2,1)}), bf16[8,2,5120]{2,1,0:T(2,128)(2,1)S(1)}, u32[]{:S(2)}, u32[]{:S(2)}) async-start(bf16[8,2,5120]{2,1,0:T(2,128)(2,1)} %broadcast_in_dim.109), calls=%async_computation.3 | async-start | bytes 327680 | tf_op jit(solution)/shard_map/all_to_all | solution.py:27
  96.1 5.7 %collective-permute-start.2 = (bf16[1,16,640]{2,1,0:T(8,128)(2,1)S(1)}, bf16[1,16,640]{2,1,0:T(8,128)(2,1)S(1)}, u32[]{:S(2)}, u32[]{:S(2)}) collective-permute-start(bf16[1,16,640]{2,1,0:T(8,128)(2,1)S(1)} %get-tuple-element.20.refs_1_), channel_id=1, source_target_pairs={{0,64},{64,0},{1,65},{65,1},{2,66},{66,2},{3,67},{67,3},{4,68},{68... | collective-permute-start | bytes 61448 | tf_op jit(solution)/shard_map/ppermute | solution.py:39
  101.8 25.4 %copy-start.9 = (s32[4,20]{1,0:T(4,128)S(1)}, s32[4,20]{1,0:T(4,128)}, u32[]{:S(2)}) copy-start(s32[4,20]{1,0:T(4,128)} %param.27) | copy-start | bytes 964
  105.7 14.5 %all-to-all-start.4 = ((bf16[8,16,1280]{2,1,0:T(8,128)(2,1)}), bf16[8,16,1280]{2,1,0:T(8,128)(2,1)S(1)}, u32[]{:S(2)}, u32[]{:S(2)}) async-start(bf16[8,16,1280]{2,1,0:T(8,128)(2,1)} %get-tuple-element.21), calls=%async_computation.4 | async-start | bytes 655360 | tf_op jit(solution)/shard_map/all_to_all | solution.py:27
  121.0 11.4 %all-to-all-start.5 = ((bf16[4,16,1280]{2,1,0:T(8,128)(2,1)}), bf16[4,16,1280]{2,1,0:T(8,128)(2,1)S(1)}, u32[]{:S(2)}, u32[]{:S(2)}) async-start(bf16[4,16,1280]{2,1,0:T(8,128)(2,1)} %shard_map.178), calls=%async_computation.5 | async-start | bytes 327680 | tf_op jit(solution)/shard_map/all_to_all | solution.py:27
  135.8 9.4 %all-to-all-start.6 = ((bf16[4,16,640]{2,1,0:T(8,128)(2,1)}), bf16[4,16,640]{2,1,0:T(8,128)(2,1)S(1)}, u32[]{:S(2)}, u32[]{:S(2)}) async-start(bf16[4,16,640]{2,1,0:T(8,128)(2,1)} %get-tuple-element.23), calls=%async_computation.6 | async-start | bytes 163840 | tf_op jit(solution)/shard_map/all_to_all | solution.py:27
  164.0 15.0 %all-to-all-start.8 = ((bf16[8,16,640]{2,1,0:T(8,128)(2,1)}), bf16[8,16,640]{2,1,0:T(8,128)(2,1)S(1)}, u32[]{:S(2)}, u32[]{:S(2)}) async-start(bf16[8,16,640]{2,1,0:T(8,128)(2,1)} %shard_map.181), calls=%async_computation.8 | async-start | bytes 327680 | tf_op jit(solution)/shard_map/all_to_all | solution.py:27
  182.1 12.7 %all-to-all-start.9 = ((bf16[8,16,640]{2,1,0:T(8,128)(2,1)}), bf16[8,16,640]{2,1,0:T(8,128)(2,1)S(1)}, u32[]{:S(2)}, u32[]{:S(2)}) async-start(bf16[8,16,640]{2,1,0:T(8,128)(2,1)} %shard_map.182), calls=%async_computation.9 | async-start | bytes 327680 | tf_op jit(solution)/shard_map/all_to_all | solution.py:27
  209.6 12.7 %all-to-all-start.11 = ((bf16[8,16,640]{2,1,0:T(8,128)(2,1)}), bf16[8,16,640]{2,1,0:T(8,128)(2,1)S(1)}, u32[]{:S(2)}, u32[]{:S(2)}) async-start(bf16[8,16,640]{2,1,0:T(8,128)(2,1)} %shard_map.184), calls=%async_computation.11 | async-start | bytes 327680 | tf_op jit(solution)/shard_map/all_to_all | solution.py:27
  236.7 14.5 %all-to-all-start.13 = ((bf16[8,16,1280]{2,1,0:T(8,128)(2,1)}), bf16[8,16,1280]{2,1,0:T(8,128)(2,1)S(1)}, u32[]{:S(2)}, u32[]{:S(2)}) async-start(bf16[8,16,1280]{2,1,0:T(8,128)(2,1)} %shard_map.186), calls=%async_computation.13 | async-start | bytes 655360 | tf_op jit(solution)/shard_map/all_to_all | solution.py:27
  252.0 10.0 %all-to-all-start.14 = ((bf16[4,16,1920]{2,1,0:T(8,128)(2,1)}), bf16[4,16,1920]{2,1,0:T(8,128)(2,1)S(1)}, u32[]{:S(2)}, u32[]{:S(2)}) async-start(bf16[4,16,1920]{2,1,0:T(8,128)(2,1)} %shard_map.187), calls=%async_computation.14 | async-start | bytes 491520 | tf_op jit(solution)/shard_map/all_to_all | solution.py:27
  265.1 5.7 %collective-permute-start.3 = (bf16[1,16,640]{2,1,0:T(8,128)(2,1)S(1)}, bf16[1,16,640]{2,1,0:T(8,128)(2,1)S(1)}, u32[]{:S(2)}, u32[]{:S(2)}) collective-permute-start(bf16[1,16,640]{2,1,0:T(8,128)(2,1)S(1)} %get-tuple-element.30.refs_0_), channel_id=1, source_target_pairs={{0,64},{64,0},{1,65},{65,1},{2,66},{66,2},{3,67},{67,3},{4,68},{68... | collective-permute-start | bytes 61448 | tf_op jit(solution)/shard_map/ppermute | solution.py:39
  276.4 12.4 %all-to-all-start.15 = ((bf16[16,2,2560]{2,1,0:T(2,128)(2,1)}), bf16[16,2,2560]{2,1,0:T(2,128)(2,1)S(1)}, u32[]{:S(2)}, u32[]{:S(2)}) async-start(bf16[16,2,2560]{2,1,0:T(2,128)(2,1)} %pad_maximum_fusion.3), calls=%async_computation.15 | async-start | bytes 327680 | tf_op jit(solution)/shard_map/all_to_all | solution.py:27
  290.4 12.3 %all-to-all-start.16 = ((bf16[8,2,2560]{2,1,0:T(2,128)(2,1)}), bf16[8,2,2560]{2,1,0:T(2,128)(2,1)S(1)}, u32[]{:S(2)}, u32[]{:S(2)}) async-start(bf16[8,2,2560]{2,1,0:T(2,128)(2,1)} %broadcast_in_dim.110), calls=%async_computation.16 | async-start | bytes 163840 | tf_op jit(solution)/shard_map/all_to_all | solution.py:27
  306.7 11.0 %all-to-all-start.17 = ((bf16[8,18,640]{2,1,0:T(8,128)(2,1)}), bf16[8,18,640]{2,1,0:T(8,128)(2,1)S(1)}, u32[]{:S(2)}, u32[]{:S(2)}) async-start(bf16[8,18,640]{2,1,0:T(8,128)(2,1)} %pad_maximum_fusion.2), calls=%async_computation.17 | async-start | bytes 491520 | tf_op jit(solution)/shard_map/all_to_all | solution.py:27
  320.4 13.0 %all-to-all-start.18 = ((bf16[8,16,640]{2,1,0:T(8,128)(2,1)}), bf16[8,16,640]{2,1,0:T(8,128)(2,1)S(1)}, u32[]{:S(2)}, u32[]{:S(2)}) async-start(bf16[8,16,640]{2,1,0:T(8,128)(2,1)} %bitcast.47), calls=%async_computation.18 | async-start | bytes 327680 | tf_op jit(solution)/shard_map/all_to_all | solution.py:27
  (9 other events, 61.4 us)
Sparse Core Ops, SparseCore 0:
  10.1 70.8 all-gather.6
  83.1 47.6 all-gather.8
  132.9 47.4 all-gather.10

commit v2 on v1

--- a/solution.py
+++ b/solution.py
@@ -46,13 +46,16 @@
 
 
 def multiply(pieces, matrix_ref, start, span, contract):
-    dims = (((1,), (contract,)), ((), ()))
     total = None
     for part, piece in enumerate(pieces):
         matrix = matrix_ref[start : start + span, part].reshape(ROWS, ROWS)
-        term = lax.dot_general(piece, matrix, dims, preferred_element_type=jnp.float32)
+        if contract == 0:
+            term = jnp.dot(piece, matrix, preferred_element_type=jnp.float32)
+        else:
+            dims = (((1,), (1,)), ((), ()))
+            term = lax.dot_general(matrix, piece, dims, preferred_element_type=jnp.float32)
         total = term if total is None else total + term
-    return total
+    return total if contract == 0 else total.T
 
 
 def bring(pack_ref, matrix_ref, sems, rows, offset):
@@ -250,8 +253,9 @@
 
 def pair_dot(vector, other, matrix):
     dims = (((1,), (1,)), ((), ()))
-    one = lax.dot_general(vector, matrix[0], dims, preferred_element_type=jnp.float32)
-    return one + lax.dot_general(other, matrix[1], dims, preferred_element_type=jnp.float32)
+    one = lax.dot_general(matrix[0], vector, dims, preferred_element_type=jnp.float32)
+    two = lax.dot_general(matrix[1], other, dims, preferred_element_type=jnp.float32)
+    return (one + two).T
 
 
 def fetch(own_ref, matrix_ref, sem):
@@ -261,9 +265,12 @@
 
 
 def lower_pivots_kernel(
-    info_ref, every_ref, own_ref, other_ref, out_ref, matrix_ref, sem
+    info_ref, every_ref, own_ref, other_ref, out_ref, matrix_ref, sems
 ):
-    fetched = fetch(own_ref, matrix_ref, sem)
+    fetched = [
+        fetch(own_ref, matrix_ref.at[0], sems.at[0]),
+        fetch(other_ref, matrix_ref.at[1], sems.at[1]),
+    ]
     place = lax.broadcasted_iota(jnp.int32, (64, ROWS), 1) // BLOCK
     sides = []
     for side in range(2):
@@ -277,11 +284,11 @@
     extra = jnp.dot(order, every_ref[:, ROWS:], preferred_element_type=jnp.float32)
     extra = extra.astype(jnp.bfloat16)
     total = None
-    for side in (1, 0):
+    for side in range(2):
         vector = vectors[side].astype(jnp.bfloat16)
-        if side == 0:
-            fetched.wait()
-        term = pair_dot(vector, crossed(vector), (matrix_ref, other_ref)[side])
+        turn = crossed(vector)
+        fetched[side].wait()
+        term = pair_dot(vector, turn, matrix_ref[side])
         total = term if total is None else total + term
     total = total.astype(jnp.bfloat16)
     for copy in range(4):
@@ -293,20 +300,23 @@
     return pl.pallas_call(
         lower_pivots_kernel,
         out_shape=jax.ShapeDtypeStruct((4, 96, ROWS), jnp.bfloat16),
-        in_specs=[smem(), vmem(), hbm(), vmem()],
+        in_specs=[smem(), vmem(), hbm(), hbm()],
         out_specs=vmem(),
         scratch_shapes=[
-            pltpu.VMEM(own.shape, jnp.bfloat16),
-            pltpu.SemaphoreType.DMA,
+            pltpu.VMEM((2,) + own.shape, jnp.bfloat16),
+            pltpu.SemaphoreType.DMA((2,)),
         ],
         compiler_params=params(),
-    )(info, every, in_hbm(own), other)
+    )(info, every, in_hbm(own), in_hbm(other))
 
 
 def lower_updates_kernel(
-    info_ref, got_ref, own_ref, other_ref, out_ref, solved_ref, matrix_ref, sem
+    info_ref, got_ref, own_ref, other_ref, out_ref, solved_ref, matrix_ref, sems
 ):
-    fetched = fetch(own_ref, matrix_ref, sem)
+    fetched = [
+        fetch(own_ref, matrix_ref.at[0], sems.at[0]),
+        fetch(other_ref, matrix_ref.at[1], sems.at[1]),
+    ]
     total = None
     for copy in range(4):
         term = got_ref[copy, :64].astype(jnp.float32)
@@ -319,9 +329,10 @@
     order = (lax.broadcasted_iota(jnp.int32, (64, 64), 1) == source).astype(jnp.bfloat16)
     vector = jnp.dot(order, vector, preferred_element_type=jnp.float32).astype(jnp.bfloat16)
     turn = crossed(vector)
-    other = pair_dot(vector, turn, other_ref)
-    fetched.wait()
-    sides = [pair_dot(vector, turn, matrix_ref), other]
+    sides = []
+    for side in range(2):
+        fetched[side].wait()
+        sides.append(pair_dot(vector, turn, matrix_ref[side]))
     even = info_ref[1] == 0
     own = sides[0].shape[1]
     first = jnp.where(even, sides[0], sides[1]).astype(jnp.bfloat16)
@@ -338,14 +349,14 @@
             jax.ShapeDtypeStruct((2, 64, ROWS), jnp.bfloat16),
             jax.ShapeDtypeStruct((64, ROWS), jnp.bfloat16),
         ],
-        in_specs=[smem(), vmem(), hbm(), vmem()],
+        in_specs=[smem(), vmem(), hbm(), hbm()],
         out_specs=[vmem()] * 2,
         scratch_shapes=[
-            pltpu.VMEM(own.shape, jnp.bfloat16),
-            pltpu.SemaphoreType.DMA,
+            pltpu.VMEM((2,) + own.shape, jnp.bfloat16),
+            pltpu.SemaphoreType.DMA((2,)),
         ],
         compiler_params=params(),
-    )(info, got, in_hbm(own), other)
+    )(info, got, in_hbm(own), in_hbm(other))
 
 
 def hand_kernel(masked, added, tailed, *refs):
@@ -455,13 +466,12 @@
 
     packs = [
         jnp.concatenate([inverse_middle.swapaxes(1, 2), coupling_middle], 1),
-        jnp.concatenate(
-            [inverse_upper.swapaxes(1, 2), coupling_upper, inverse_root.swapaxes(1, 2)], 1
-        ),
+        jnp.concatenate([inverse_upper.swapaxes(1, 2), coupling_upper], 1),
+        inverse_root.swapaxes(1, 2),
         coupling_lower,
     ]
     packs = [lax.all_gather(pack, SHARE, axis=0, tiled=False) for pack in packs]
-    pivot_at = {2: (packs[0], 320, 0), 1: (packs[1], 160, 0), 0: (packs[1], 80, 3)}
+    pivot_at = {2: (packs[0], 320, 0), 1: (packs[1], 160, 0), 0: (packs[2], 80, 0)}
     update_at = {2: (packs[0], 160, 2), 1: (packs[1], 80, 2)}
 
     def front_of(level):
@@ -613,7 +623,7 @@
     both = jnp.concatenate([both.astype(jnp.float32), passed], 2)
     handed = take_blocks(handing(), both).astype(jnp.bfloat16)
     vector = gather(handed, "panel", PANELS).transpose(1, 0, 2).reshape(16, U)
-    (partial,) = over_columns(packs[2], 320, 0, 1, base=vector, dtype=jnp.float32)
+    (partial,) = over_columns(packs[3], 320, 0, 1, base=vector, dtype=jnp.float32)
     target = (solved_mine.astype(jnp.float32) - partial[0]).astype(jnp.bfloat16)
     smaller = [answer.reshape(2, SHARES, -1).transpose(1, 0, 2) for answer in answers]
     counts = [piece.shape[2] for piece in smaller]

time: 344 us -> 340 us (0.988)
  blocking collectives: 35.9 us -> 31.8 us
    all_to_all x3, blocking collectives: 35.9 us -> 31.8 us  [exchange(): return lax.all_to_all(value, axes, 0, 0, tiled=True)]
  transfers between devices with their start and end apart: 23 -> 24, of which waited for: 19 -> 18; matrix products, arithmetic and copies ran while one was open for 5% -> 5% of each run, Pallas kernels for 13% -> 13%
where the time goes in v2:
time: 340 us; the launch traced here: 337 us
  waiting for transfers between devices  134 us (39%)
  starting transfers between devices  84.4 us (25%)
  Pallas kernels  48.3 us (14%)
  blocking collectives  31.8 us (9%)
  between operations  19.8 us (6%)
  local copies, waits for them, and re-layouts  9.78 us (3%)
  other arithmetic  9.6 us (3%)
    all_to_all x16, waiting for transfers between devices, exchange(): return lax.all_to_all(value, axes, 0, 0, tiled=True)  128 us
    all_to_all x16, starting transfers between devices, exchange(): return lax.all_to_all(value, axes, 0, 0, tiled=True)  74.4 us
    all_to_all x3, blocking collectives, exchange(): return lax.all_to_all(value, axes, 0, 0, tiled=True)  31.8 us
    pallas_call x6, Pallas kernels, over_columns(): pl.pallas_call(functools.partial(columns_kernel, rows, offset, updates, h...  19.2 us
    pallas_call x5, Pallas kernels, over_rows(): pl.pallas_call(functools.partial(rows_kernel, rows, offset, len(parts), m...  15.2 us
  transfers between devices with their start and end apart: 24, of which 18 were waited for; matrix products, arithmetic and copies ran while one was open for 5% of the time, Pallas kernels for 13%

profile of v2, /device:TPU:6, one launch (start us, length us, event | category | flops | bytes accessed | tf_op | source)
XLA Modules:
  0.0 337.2 jit_solution(3296290479624927676)
XLA Ops:
  15.1 7.3 %all-to-all-start = ((bf16[16,8,1280]{2,1,0:T(8,128)(2,1)}), bf16[16,8,1280]{2,1,0:T(8,128)(2,1)S(1)}, u32[]{:S(2)}, u32[]{:S(2)}) async-start(bf16[16,8,1280]{2,1,0:T(8,128)(2,1)} %bitcast.6), calls=%async_computation | async-start | bytes 655360 | tf_op jit(solution)/shard_map/all_to_all | solution.py:27
  26.2 8.1 %all-to-all-done = bf16[16,8,1280]{2,1,0:T(8,128)(2,1)S(1)} async-done(((bf16[16,8,1280]{2,1,0:T(8,128)(2,1)}), bf16[16,8,1280]{2,1,0:T(8,128)(2,1)S(1)}, u32[]{:S(2)}, u32[]{:S(2)}) %all-to-all-start) | async-done | bytes 327712 | tf_op jit(solution)/shard_map/all_to_all | solution.py:27
  38.4 5.5 %all-to-all-start.1 = ((bf16[4,96,640]{2,1,0:T(8,128)(2,1)}), bf16[4,96,640]{2,1,0:T(8,128)(2,1)S(1)}, u32[]{:S(2)}, u32[]{:S(2)}) async-start(bf16[4,96,640]{2,1,0:T(8,128)(2,1)} %shard_map.174), calls=%async_computation.1 | async-start | bytes 983040 | tf_op jit(solution)/shard_map/all_to_all | solution.py:27
  44.7 12.4 %all-to-all-done.1.got_ref = bf16[4,96,640]{2,1,0:T(8,128)(2,1)S(1)} async-done(((bf16[4,96,640]{2,1,0:T(8,128)(2,1)}), bf16[4,96,640]{2,1,0:T(8,128)(2,1)S(1)}, u32[]{:S(2)}, u32[]{:S(2)}) %all-to-all-start.1) | async-done | bytes 491552 | tf_op jit(solution)/shard_map/all_to_all | solution.py:27
  60.5 8.7 %all-to-all-start.2 = ((bf16[64,2,640]{2,1,0:T(2,128)(2,1)}), bf16[64,2,640]{2,1,0:T(2,128)(2,1)S(1)}, u32[]{:S(2)}, u32[]{:S(2)}) async-start(bf16[64,2,640]{2,1,0:T(2,128)(2,1)} %reshape.188), calls=%async_computation.2 | async-start | bytes 327680 | tf_op jit(solution)/shard_map/all_to_all | solution.py:27
  69.9 9.7 %all-to-all-done.2 = bf16[64,2,640]{2,1,0:T(2,128)(2,1)S(1)} async-done(((bf16[64,2,640]{2,1,0:T(2,128)(2,1)}), bf16[64,2,640]{2,1,0:T(2,128)(2,1)S(1)}, u32[]{:S(2)}, u32[]{:S(2)}) %all-to-all-start.2) | async-done | bytes 163872 | tf_op jit(solution)/shard_map/all_to_all | solution.py:27
  85.3 8.0 %all-to-all-done.3 = bf16[8,2,5120]{2,1,0:T(2,128)(2,1)S(1)} async-done(((bf16[8,2,5120]{2,1,0:T(2,128)(2,1)}), bf16[8,2,5120]{2,1,0:T(2,128)(2,1)S(1)}, u32[]{:S(2)}, u32[]{:S(2)}) %all-to-all-start.3) | async-done | bytes 163872 | tf_op jit(solution)/shard_map/all_to_all | solution.py:27
  109.8 11.1 %all-to-all-done.4.refs_0_ = bf16[8,16,1280]{2,1,0:T(8,128)(2,1)S(1)} async-done(((bf16[8,16,1280]{2,1,0:T(8,128)(2,1)}), bf16[8,16,1280]{2,1,0:T(8,128)(2,1)S(1)}, u32[]{:S(2)}, u32[]{:S(2)}) %all-to-all-start.4) | async-done | bytes 327712 | tf_op jit(solution)/shard_map/all_to_all | solution.py:27
  121.6 5.3 %all-to-all-start.5 = ((bf16[4,16,1280]{2,1,0:T(8,128)(2,1)}), bf16[4,16,1280]{2,1,0:T(8,128)(2,1)S(1)}, u32[]{:S(2)}, u32[]{:S(2)}) async-start(bf16[4,16,1280]{2,1,0:T(8,128)(2,1)} %shard_map.178), calls=%async_computation.5 | async-start | bytes 327680 | tf_op jit(solution)/shard_map/all_to_all | solution.py:27
  140.3 5.1 %all-to-all-done.6.refs_1_ = bf16[4,16,640]{2,1,0:T(8,128)(2,1)S(1)} async-done(((bf16[4,16,640]{2,1,0:T(8,128)(2,1)}), bf16[4,16,640]{2,1,0:T(8,128)(2,1)S(1)}, u32[]{:S(2)}, u32[]{:S(2)}) %all-to-all-start.6) | async-done | bytes 81952 | tf_op jit(solution)/shard_map/all_to_all | solution.py:27
  147.6 11.8 %all_to_all.95.refs_0_ = bf16[8,16,640]{2,1,0:T(8,128)(2,1)S(1)} all-to-all(bf16[8,16,640]{2,1,0:T(8,128)(2,1)S(1)} %get-tuple-element.24), channel_id=1, replica_groups=mesh['z2'=2,'z1'=2,'z0'=2,'x'=4,'c'=2,'panel'=8] {'panel'}, dimensions={0} | all-to-all | bytes 327680 | tf_op jit(solution)/shard_map/all_to_all | solution.py:27
  160.1 7.9 %all-to-all-start.8 = ((bf16[8,16,640]{2,1,0:T(8,128)(2,1)}), bf16[8,16,640]{2,1,0:T(8,128)(2,1)S(1)}, u32[]{:S(2)}, u32[]{:S(2)}) async-start(bf16[8,16,640]{2,1,0:T(8,128)(2,1)} %shard_map.181), calls=%async_computation.8 | async-start | bytes 327680 | tf_op jit(solution)/shard_map/all_to_all | solution.py:27
  169.3 8.2 %all-to-all-done.8.refs_2_ = bf16[8,16,640]{2,1,0:T(8,128)(2,1)S(1)} async-done(((bf16[8,16,640]{2,1,0:T(8,128)(2,1)}), bf16[8,16,640]{2,1,0:T(8,128)(2,1)S(1)}, u32[]{:S(2)}, u32[]{:S(2)}) %all-to-all-start.8) | async-done | bytes 163872 | tf_op jit(solution)/shard_map/all_to_all | solution.py:27
  184.6 8.7 %all-to-all-done.9.refs_1_ = bf16[8,16,640]{2,1,0:T(8,128)(2,1)S(1)} async-done(((bf16[8,16,640]{2,1,0:T(8,128)(2,1)}), bf16[8,16,640]{2,1,0:T(8,128)(2,1)S(1)}, u32[]{:S(2)}, u32[]{:S(2)}) %all-to-all-start.9) | async-done | bytes 163872 | tf_op jit(solution)/shard_map/all_to_all | solution.py:27
  195.6 11.8 %all_to_all.96.refs_1_ = bf16[8,16,640]{2,1,0:T(8,128)(2,1)S(1)} all-to-all(bf16[8,16,640]{2,1,0:T(8,128)(2,1)S(1)} %get-tuple-element.26), channel_id=1, replica_groups=mesh['z2'=2,'z1'=2,'z0'=2,'x'=4,'c'=2,'panel'=8] {'panel'}, dimensions={0} | all-to-all | bytes 327680 | tf_op jit(solution)/shard_map/all_to_all | solution.py:27
  211.6 9.0 %all-to-all-done.11.refs_1_ = bf16[8,16,640]{2,1,0:T(8,128)(2,1)S(1)} async-done(((bf16[8,16,640]{2,1,0:T(8,128)(2,1)}), bf16[8,16,640]{2,1,0:T(8,128)(2,1)S(1)}, u32[]{:S(2)}, u32[]{:S(2)}) %all-to-all-start.11) | async-done | bytes 163872 | tf_op jit(solution)/shard_map/all_to_all | solution.py:27
  223.1 8.2 %all_to_all.97.refs_0_ = bf16[4,16,640]{2,1,0:T(8,128)(2,1)S(1)} all-to-all(bf16[4,16,640]{2,1,0:T(8,128)(2,1)S(1)} %get-tuple-element.27), channel_id=1, replica_groups=mesh['z2'=2,'z1'=2,'z0'=2,'x'=4,'c'=2,'panel'=8] {'z1','z0'}, dimensions={0} | all-to-all | bytes 163840 | tf_op jit(solution)/shard_map/all_to_all | solution.py:27
  238.9 10.2 %all-to-all-done.13.refs_1_ = bf16[8,16,1280]{2,1,0:T(8,128)(2,1)S(1)} async-done(((bf16[8,16,1280]{2,1,0:T(8,128)(2,1)}), bf16[8,16,1280]{2,1,0:T(8,128)(2,1)S(1)}, u32[]{:S(2)}, u32[]{:S(2)}) %all-to-all-start.13) | async-done | bytes 327712 | tf_op jit(solution)/shard_map/all_to_all | solution.py:27
  254.1 5.8 %all-to-all-done.14.refs_1_.held_ref = bf16[4,16,1920]{2,1,0:T(8,128)(2,1)S(1)} async-done(((bf16[4,16,1920]{2,1,0:T(8,128)(2,1)}), bf16[4,16,1920]{2,1,0:T(8,128)(2,1)S(1)}, u32[]{:S(2)}, u32[]{:S(2)}) %all-to-all-start.14) | async-done | bytes 245792 | tf_op jit(solution)/shard_map/all_to_all | solution.py:27
  278.8 6.9 %all-to-all-done.15 = bf16[16,2,2560]{2,1,0:T(2,128)(2,1)S(1)} async-done(((bf16[16,2,2560]{2,1,0:T(2,128)(2,1)}), bf16[16,2,2560]{2,1,0:T(2,128)(2,1)S(1)}, u32[]{:S(2)}, u32[]{:S(2)}) %all-to-all-start.15) | async-done | bytes 163872 | tf_op jit(solution)/shard_map/all_to_all | solution.py:27
  290.9 8.3 %all-to-all-done.16 = bf16[8,2,2560]{2,1,0:T(2,128)(2,1)S(1)} async-done(((bf16[8,2,2560]{2,1,0:T(2,128)(2,1)}), bf16[8,2,2560]{2,1,0:T(2,128)(2,1)S(1)}, u32[]{:S(2)}, u32[]{:S(2)}) %all-to-all-start.16) | async-done | bytes 81952 | tf_op jit(solution)/shard_map/all_to_all | solution.py:27
  303.3 5.7 %all-to-all-start.17 = ((bf16[8,18,640]{2,1,0:T(8,128)(2,1)}), bf16[8,18,640]{2,1,0:T(8,128)(2,1)S(1)}, u32[]{:S(2)}, u32[]{:S(2)}) async-start(bf16[8,18,640]{2,1,0:T(8,128)(2,1)} %pad_maximum_fusion.2), calls=%async_computation.17 | async-start | bytes 491520 | tf_op jit(solution)/shard_map/all_to_all | solution.py:27
  309.0 5.3 %all-to-all-done.17.got_ref = bf16[8,18,640]{2,1,0:T(8,128)(2,1)S(1)} async-done(((bf16[8,18,640]{2,1,0:T(8,128)(2,1)}), bf16[8,18,640]{2,1,0:T(8,128)(2,1)S(1)}, u32[]{:S(2)}, u32[]{:S(2)}) %all-to-all-start.17) | async-done | bytes 184352 | tf_op jit(solution)/shard_map/all_to_all | solution.py:27
  323.1 6.9 %all-to-all-done.18 = bf16[8,16,640]{2,1,0:T(8,128)(2,1)S(1)} async-done(((bf16[8,16,640]{2,1,0:T(8,128)(2,1)}), bf16[8,16,640]{2,1,0:T(8,128)(2,1)S(1)}, u32[]{:S(2)}, u32[]{:S(2)}) %all-to-all-start.18) | async-done | bytes 163872 | tf_op jit(solution)/shard_map/all_to_all | solution.py:27
  (156 shorter events, 121.6 us)
Async XLA Ops:
  7.2 86.1 %all-gather.9.cloned.1.call-start = ((), (), s32[]{:S(2)}) async-start(), calls=%async_computation.19 | async-start | bytes 11059200 | tf_op jit(solution)/shard_map/all_gather | solution.py:473
  9.9 118.6 %all-gather.11.cloned.1.call-start = ((), (), s32[]{:S(2)}) async-start(), calls=%async_computation.20 | async-start | bytes 5529600 | tf_op jit(solution)/shard_map/all_gather | solution.py:473
  10.9 158.4 %all-gather.13.cloned.1.call-start = ((), (), s32[]{:S(2)}) async-start(), calls=%async_computation.21 | async-start | bytes 1843200 | tf_op jit(solution)/shard_map/all_gather | solution.py:473
  11.6 287.6 %all-gather.15.cloned.1.call-start = ((), (), s32[]{:S(2)}) async-start(), calls=%async_computation.22 | async-start | bytes 7372800 | tf_op jit(solution)/shard_map/all_gather | solution.py:473
  12.2 22.1 %collective-permute-start = (bf16[2,640,640]{2,1,0:T(8,128)(2,1)S(1)}, bf16[2,640,640]{2,1,0:T(8,128)(2,1)}, u32[]{:S(2)}, u32[]{:S(2)}) collective-permute-start(bf16[2,640,640]{2,1,0:T(8,128)(2,1)S(1)} %copy-done), channel_id=1, source_target_pairs={{0,8},{8,0},{1,9},{9,1},{2,10},{10,2},{3,11},{11,3},{4,12},{12,4},... | collective-permute-start | bytes 4915208 | tf_op jit(solution)/shard_map/ppermute | solution.py:529
  15.1 19.2 %all-to-all-start = ((bf16[16,8,1280]{2,1,0:T(8,128)(2,1)}), bf16[16,8,1280]{2,1,0:T(8,128)(2,1)S(1)}, u32[]{:S(2)}, u32[]{:S(2)}) async-start(bf16[16,8,1280]{2,1,0:T(8,128)(2,1)} %bitcast.6), calls=%async_computation | async-start | bytes 655360 | tf_op jit(solution)/shard_map/all_to_all | solution.py:27
  22.4 22.2 %collective-permute-start.1 = (bf16[2,320,640]{2,1,0:T(8,128)(2,1)S(1)}, bf16[2,320,640]{2,1,0:T(8,128)(2,1)}, u32[]{:S(2)}, u32[]{:S(2)}) collective-permute-start(bf16[2,320,640]{2,1,0:T(8,128)(2,1)S(1)} %copy-done.1), channel_id=1, source_target_pairs={{0,8},{8,0},{1,9},{9,1},{2,10},{10,2},{3,11},{11,3},{4,12},{12,4},... | collective-permute-start | bytes 2457608 | tf_op jit(solution)/shard_map/ppermute | solution.py:530
  38.4 18.6 %all-to-all-start.1 = ((bf16[4,96,640]{2,1,0:T(8,128)(2,1)}), bf16[4,96,640]{2,1,0:T(8,128)(2,1)S(1)}, u32[]{:S(2)}, u32[]{:S(2)}) async-start(bf16[4,96,640]{2,1,0:T(8,128)(2,1)} %shard_map.174), calls=%async_computation.1 | async-start | bytes 983040 | tf_op jit(solution)/shard_map/all_to_all | solution.py:27
  60.5 19.1 %all-to-all-start.2 = ((bf16[64,2,640]{2,1,0:T(2,128)(2,1)}), bf16[64,2,640]{2,1,0:T(2,128)(2,1)S(1)}, u32[]{:S(2)}, u32[]{:S(2)}) async-start(bf16[64,2,640]{2,1,0:T(2,128)(2,1)} %reshape.188), calls=%async_computation.2 | async-start | bytes 327680 | tf_op jit(solution)/shard_map/all_to_all | solution.py:27
  80.5 12.7 %all-to-all-start.3 = ((bf16[8,2,5120]{2,1,0:T(2,128)(2,1)}), bf16[8,2,5120]{2,1,0:T(2,128)(2,1)S(1)}, u32[]{:S(2)}, u32[]{:S(2)}) async-start(bf16[8,2,5120]{2,1,0:T(2,128)(2,1)} %broadcast_in_dim.109), calls=%async_computation.3 | async-start | bytes 327680 | tf_op jit(solution)/shard_map/all_to_all | solution.py:27
  97.2 5.7 %collective-permute-start.2 = (bf16[1,16,640]{2,1,0:T(8,128)(2,1)S(1)}, bf16[1,16,640]{2,1,0:T(8,128)(2,1)S(1)}, u32[]{:S(2)}, u32[]{:S(2)}) collective-permute-start(bf16[1,16,640]{2,1,0:T(8,128)(2,1)S(1)} %get-tuple-element.20.refs_1_), channel_id=1, source_target_pairs={{0,64},{64,0},{1,65},{65,1},{2,66},{66,2},{3,67},{67,3},{4,68},{68... | collective-permute-start | bytes 61448 | tf_op jit(solution)/shard_map/ppermute | solution.py:39
  106.3 14.6 %all-to-all-start.4 = ((bf16[8,16,1280]{2,1,0:T(8,128)(2,1)}), bf16[8,16,1280]{2,1,0:T(8,128)(2,1)S(1)}, u32[]{:S(2)}, u32[]{:S(2)}) async-start(bf16[8,16,1280]{2,1,0:T(8,128)(2,1)} %get-tuple-element.21), calls=%async_computation.4 | async-start | bytes 655360 | tf_op jit(solution)/shard_map/all_to_all | solution.py:27
  121.6 11.3 %all-to-all-start.5 = ((bf16[4,16,1280]{2,1,0:T(8,128)(2,1)}), bf16[4,16,1280]{2,1,0:T(8,128)(2,1)S(1)}, u32[]{:S(2)}, u32[]{:S(2)}) async-start(bf16[4,16,1280]{2,1,0:T(8,128)(2,1)} %shard_map.178), calls=%async_computation.5 | async-start | bytes 327680 | tf_op jit(solution)/shard_map/all_to_all | solution.py:27
  136.3 9.1 %all-to-all-start.6 = ((bf16[4,16,640]{2,1,0:T(8,128)(2,1)}), bf16[4,16,640]{2,1,0:T(8,128)(2,1)S(1)}, u32[]{:S(2)}, u32[]{:S(2)}) async-start(bf16[4,16,640]{2,1,0:T(8,128)(2,1)} %get-tuple-element.23), calls=%async_computation.6 | async-start | bytes 163840 | tf_op jit(solution)/shard_map/all_to_all | solution.py:27
  160.1 17.3 %all-to-all-start.8 = ((bf16[8,16,640]{2,1,0:T(8,128)(2,1)}), bf16[8,16,640]{2,1,0:T(8,128)(2,1)S(1)}, u32[]{:S(2)}, u32[]{:S(2)}) async-start(bf16[8,16,640]{2,1,0:T(8,128)(2,1)} %shard_map.181), calls=%async_computation.8 | async-start | bytes 327680 | tf_op jit(solution)/shard_map/all_to_all | solution.py:27
  180.6 12.8 %all-to-all-start.9 = ((bf16[8,16,640]{2,1,0:T(8,128)(2,1)}), bf16[8,16,640]{2,1,0:T(8,128)(2,1)S(1)}, u32[]{:S(2)}, u32[]{:S(2)}) async-start(bf16[8,16,640]{2,1,0:T(8,128)(2,1)} %shard_map.182), calls=%async_computation.9 | async-start | bytes 327680 | tf_op jit(solution)/shard_map/all_to_all | solution.py:27
  208.1 12.5 %all-to-all-start.11 = ((bf16[8,16,640]{2,1,0:T(8,128)(2,1)}), bf16[8,16,640]{2,1,0:T(8,128)(2,1)S(1)}, u32[]{:S(2)}, u32[]{:S(2)}) async-start(bf16[8,16,640]{2,1,0:T(8,128)(2,1)} %shard_map.184), calls=%async_computation.11 | async-start | bytes 327680 | tf_op jit(solution)/shard_map/all_to_all | solution.py:27
  234.6 14.5 %all-to-all-start.13 = ((bf16[8,16,1280]{2,1,0:T(8,128)(2,1)}), bf16[8,16,1280]{2,1,0:T(8,128)(2,1)S(1)}, u32[]{:S(2)}, u32[]{:S(2)}) async-start(bf16[8,16,1280]{2,1,0:T(8,128)(2,1)} %shard_map.186), calls=%async_computation.13 | async-start | bytes 655360 | tf_op jit(solution)/shard_map/all_to_all | solution.py:27
  249.9 10.0 %all-to-all-start.14 = ((bf16[4,16,1920]{2,1,0:T(8,128)(2,1)}), bf16[4,16,1920]{2,1,0:T(8,128)(2,1)S(1)}, u32[]{:S(2)}, u32[]{:S(2)}) async-start(bf16[4,16,1920]{2,1,0:T(8,128)(2,1)} %shard_map.187), calls=%async_computation.14 | async-start | bytes 491520 | tf_op jit(solution)/shard_map/all_to_all | solution.py:27
  263.0 5.7 %collective-permute-start.3 = (bf16[1,16,640]{2,1,0:T(8,128)(2,1)S(1)}, bf16[1,16,640]{2,1,0:T(8,128)(2,1)S(1)}, u32[]{:S(2)}, u32[]{:S(2)}) collective-permute-start(bf16[1,16,640]{2,1,0:T(8,128)(2,1)S(1)} %get-tuple-element.30.refs_0_), channel_id=1, source_target_pairs={{0,64},{64,0},{1,65},{65,1},{2,66},{66,2},{3,67},{67,3},{4,68},{68... | collective-permute-start | bytes 61448 | tf_op jit(solution)/shard_map/ppermute | solution.py:39
  273.6 12.1 %all-to-all-start.15 = ((bf16[16,2,2560]{2,1,0:T(2,128)(2,1)}), bf16[16,2,2560]{2,1,0:T(2,128)(2,1)S(1)}, u32[]{:S(2)}, u32[]{:S(2)}) async-start(bf16[16,2,2560]{2,1,0:T(2,128)(2,1)} %pad_maximum_fusion.3), calls=%async_computation.15 | async-start | bytes 327680 | tf_op jit(solution)/shard_map/all_to_all | solution.py:27
  287.3 11.9 %all-to-all-start.16 = ((bf16[8,2,2560]{2,1,0:T(2,128)(2,1)}), bf16[8,2,2560]{2,1,0:T(2,128)(2,1)S(1)}, u32[]{:S(2)}, u32[]{:S(2)}) async-start(bf16[8,2,2560]{2,1,0:T(2,128)(2,1)} %broadcast_in_dim.110), calls=%async_computation.16 | async-start | bytes 163840 | tf_op jit(solution)/shard_map/all_to_all | solution.py:27
  303.3 11.0 %all-to-all-start.17 = ((bf16[8,18,640]{2,1,0:T(8,128)(2,1)}), bf16[8,18,640]{2,1,0:T(8,128)(2,1)S(1)}, u32[]{:S(2)}, u32[]{:S(2)}) async-start(bf16[8,18,640]{2,1,0:T(8,128)(2,1)} %pad_maximum_fusion.2), calls=%async_computation.17 | async-start | bytes 491520 | tf_op jit(solution)/shard_map/all_to_all | solution.py:27
  317.0 13.0 %all-to-all-start.18 = ((bf16[8,16,640]{2,1,0:T(8,128)(2,1)}), bf16[8,16,640]{2,1,0:T(8,128)(2,1)S(1)}, u32[]{:S(2)}, u32[]{:S(2)}) async-start(bf16[8,16,640]{2,1,0:T(8,128)(2,1)} %bitcast.48), calls=%async_computation.18 | async-start | bytes 327680 | tf_op jit(solution)/shard_map/all_to_all | solution.py:27
  (11 other events, 98.7 us)
Sparse Core Ops, SparseCore 0:
  10.1 70.8 all-gather.8
  83.1 40.7 all-gather.10
  126.1 30.2 all-gather.12
  158.4 47.0 all-gather.14

commit v3 on v2

--- a/solution.py
+++ b/solution.py
@@ -45,9 +45,11 @@
     return vector.astype(jnp.bfloat16), other.astype(jnp.bfloat16)
 
 
-def multiply(pieces, matrix_ref, start, span, contract):
+def multiply(pieces, matrix_ref, start, span, contract, copies):
     total = None
     for part, piece in enumerate(pieces):
+        for share in range(start, start + span):
+            copies[share, part].wait()
         matrix = matrix_ref[start : start + span, part].reshape(ROWS, ROWS)
         if contract == 0:
             term = jnp.dot(piece, matrix, preferred_element_type=jnp.float32)
@@ -59,17 +61,18 @@
 
 
 def bring(pack_ref, matrix_ref, sems, rows, offset):
-    copies = []
-    for share in range(SHARES):
-        copies.append(
-            pltpu.make_async_copy(
-                pack_ref.at[share, :, pl.ds(offset * rows, rows)],
-                matrix_ref.at[share],
-                sems.at[share],
-            )
-        )
-    for copy in copies:
-        copy.start()
+    group = ROWS // rows
+    copies = {}
+    for first in range(0, SHARES, group):
+        for part in range(2):
+            for share in range(first, first + group):
+                copy = pltpu.make_async_copy(
+                    pack_ref.at[share, part, pl.ds(offset * rows, rows)],
+                    matrix_ref.at[share, part],
+                    sems.at[share, part],
+                )
+                copy.start()
+                copies[share, part] = copy
     return copies
 
 
@@ -109,7 +112,7 @@
 def matrix_scratch(rows):
     return [
         pltpu.VMEM((SHARES, 2, rows, ROWS), jnp.bfloat16),
-        pltpu.SemaphoreType.DMA((SHARES,)),
+        pltpu.SemaphoreType.DMA((SHARES, 2)),
     ]
 
 
@@ -143,9 +146,7 @@
             vector = base_ref[:, step * ROWS : (step + 1) * ROWS].astype(jnp.float32)
         if keep:
             keep_ref[:, step * ROWS : (step + 1) * ROWS] = vector.astype(jnp.bfloat16)
-        for share in range(step * group, (step + 1) * group):
-            copies[share].wait()
-        term = multiply(halves(vector), matrix_ref, step * group, group, 0)
+        term = multiply(halves(vector), matrix_ref, step * group, group, 0, copies)
         total = term if total is None else total + term
     for place in range(updates):
         passed_ref[:, place * BLOCK : (place + 1) * BLOCK] = take_block(
@@ -217,9 +218,8 @@
     pieces = halves(total)
     group = ROWS // rows
     for step in range(SHARES // group):
-        for share in range(step * group, (step + 1) * group):
-            copies[share].wait()
-        result = multiply(pieces, matrix_ref, step * group, group, 1).astype(jnp.bfloat16)
+        result = multiply(pieces, matrix_ref, step * group, group, 1, copies)
+        result = result.astype(jnp.bfloat16)
         for copy in range(out_ref.shape[0]):
             out_ref[copy, :, step * ROWS : (step + 1) * ROWS] = result
 

time: 340 us -> 342 us (level)
  no operation moved by 1% of the time
where the time goes in v3:
time: 342 us; the launch traced here: 339 us
  waiting for transfers between devices  133 us (39%)
  starting transfers between devices  84.5 us (25%)
  Pallas kernels  49.7 us (15%)
  blocking collectives  31.8 us (9%)
  between operations  19.8 us (6%)
  local copies, waits for them, and re-layouts  9.78 us (3%)
  other arithmetic  9.6 us (3%)
    all_to_all x16, waiting for transfers between devices, exchange(): return lax.all_to_all(value, axes, 0, 0, tiled=True)  128 us
    all_to_all x16, starting transfers between devices, exchange(): return lax.all_to_all(value, axes, 0, 0, tiled=True)  74.5 us
    all_to_all x3, blocking collectives, exchange(): return lax.all_to_all(value, axes, 0, 0, tiled=True)  31.8 us
    pallas_call x6, Pallas kernels, over_columns(): pl.pallas_call(functools.partial(columns_kernel, rows, offset, updates, h...  19.8 us
    pallas_call x5, Pallas kernels, over_rows(): pl.pallas_call(functools.partial(rows_kernel, rows, offset, len(parts), m...  16 us
  transfers between devices with their start and end apart: 24, of which 18 were waited for; matrix products, arithmetic and copies ran while one was open for 5% of the time, Pallas kernels for 13%

profile of v3, /device:TPU:6, one launch (start us, length us, event | category | flops | bytes accessed | tf_op | source)
XLA Modules:
  0.0 338.6 jit_solution(5430584346252621688)
XLA Ops:
  15.1 7.3 %all-to-all-start = ((bf16[16,8,1280]{2,1,0:T(8,128)(2,1)}), bf16[16,8,1280]{2,1,0:T(8,128)(2,1)S(1)}, u32[]{:S(2)}, u32[]{:S(2)}) async-start(bf16[16,8,1280]{2,1,0:T(8,128)(2,1)} %bitcast.6), calls=%async_computation | async-start | bytes 655360 | tf_op jit(solution)/shard_map/all_to_all | solution.py:27
  26.2 8.1 %all-to-all-done = bf16[16,8,1280]{2,1,0:T(8,128)(2,1)S(1)} async-done(((bf16[16,8,1280]{2,1,0:T(8,128)(2,1)}), bf16[16,8,1280]{2,1,0:T(8,128)(2,1)S(1)}, u32[]{:S(2)}, u32[]{:S(2)}) %all-to-all-start) | async-done | bytes 327712 | tf_op jit(solution)/shard_map/all_to_all | solution.py:27
  38.4 5.5 %all-to-all-start.1 = ((bf16[4,96,640]{2,1,0:T(8,128)(2,1)}), bf16[4,96,640]{2,1,0:T(8,128)(2,1)S(1)}, u32[]{:S(2)}, u32[]{:S(2)}) async-start(bf16[4,96,640]{2,1,0:T(8,128)(2,1)} %shard_map.174), calls=%async_computation.1 | async-start | bytes 983040 | tf_op jit(solution)/shard_map/all_to_all | solution.py:27
  44.7 12.4 %all-to-all-done.1.got_ref = bf16[4,96,640]{2,1,0:T(8,128)(2,1)S(1)} async-done(((bf16[4,96,640]{2,1,0:T(8,128)(2,1)}), bf16[4,96,640]{2,1,0:T(8,128)(2,1)S(1)}, u32[]{:S(2)}, u32[]{:S(2)}) %all-to-all-start.1) | async-done | bytes 491552 | tf_op jit(solution)/shard_map/all_to_all | solution.py:27
  60.5 8.7 %all-to-all-start.2 = ((bf16[64,2,640]{2,1,0:T(2,128)(2,1)}), bf16[64,2,640]{2,1,0:T(2,128)(2,1)S(1)}, u32[]{:S(2)}, u32[]{:S(2)}) async-start(bf16[64,2,640]{2,1,0:T(2,128)(2,1)} %reshape.188), calls=%async_computation.2 | async-start | bytes 327680 | tf_op jit(solution)/shard_map/all_to_all | solution.py:27
  69.9 9.7 %all-to-all-done.2 = bf16[64,2,640]{2,1,0:T(2,128)(2,1)S(1)} async-done(((bf16[64,2,640]{2,1,0:T(2,128)(2,1)}), bf16[64,2,640]{2,1,0:T(2,128)(2,1)S(1)}, u32[]{:S(2)}, u32[]{:S(2)}) %all-to-all-start.2) | async-done | bytes 163872 | tf_op jit(solution)/shard_map/all_to_all | solution.py:27
  85.3 8.0 %all-to-all-done.3 = bf16[8,2,5120]{2,1,0:T(2,128)(2,1)S(1)} async-done(((bf16[8,2,5120]{2,1,0:T(2,128)(2,1)}), bf16[8,2,5120]{2,1,0:T(2,128)(2,1)S(1)}, u32[]{:S(2)}, u32[]{:S(2)}) %all-to-all-start.3) | async-done | bytes 163872 | tf_op jit(solution)/shard_map/all_to_all | solution.py:27
  110.0 11.1 %all-to-all-done.4.refs_0_ = bf16[8,16,1280]{2,1,0:T(8,128)(2,1)S(1)} async-done(((bf16[8,16,1280]{2,1,0:T(8,128)(2,1)}), bf16[8,16,1280]{2,1,0:T(8,128)(2,1)S(1)}, u32[]{:S(2)}, u32[]{:S(2)}) %all-to-all-start.4) | async-done | bytes 327712 | tf_op jit(solution)/shard_map/all_to_all | solution.py:27
  121.8 5.3 %all-to-all-start.5 = ((bf16[4,16,1280]{2,1,0:T(8,128)(2,1)}), bf16[4,16,1280]{2,1,0:T(8,128)(2,1)S(1)}, u32[]{:S(2)}, u32[]{:S(2)}) async-start(bf16[4,16,1280]{2,1,0:T(8,128)(2,1)} %shard_map.178), calls=%async_computation.5 | async-start | bytes 327680 | tf_op jit(solution)/shard_map/all_to_all | solution.py:27
  140.8 5.1 %all-to-all-done.6.refs_1_ = bf16[4,16,640]{2,1,0:T(8,128)(2,1)S(1)} async-done(((bf16[4,16,640]{2,1,0:T(8,128)(2,1)}), bf16[4,16,640]{2,1,0:T(8,128)(2,1)S(1)}, u32[]{:S(2)}, u32[]{:S(2)}) %all-to-all-start.6) | async-done | bytes 81952 | tf_op jit(solution)/shard_map/all_to_all | solution.py:27
  148.2 11.8 %all_to_all.95.refs_0_ = bf16[8,16,640]{2,1,0:T(8,128)(2,1)S(1)} all-to-all(bf16[8,16,640]{2,1,0:T(8,128)(2,1)S(1)} %get-tuple-element.24), channel_id=1, replica_groups=mesh['z2'=2,'z1'=2,'z0'=2,'x'=4,'c'=2,'panel'=8] {'panel'}, dimensions={0} | all-to-all | bytes 327680 | tf_op jit(solution)/shard_map/all_to_all | solution.py:27
  160.7 7.8 %all-to-all-start.8 = ((bf16[8,16,640]{2,1,0:T(8,128)(2,1)}), bf16[8,16,640]{2,1,0:T(8,128)(2,1)S(1)}, u32[]{:S(2)}, u32[]{:S(2)}) async-start(bf16[8,16,640]{2,1,0:T(8,128)(2,1)} %shard_map.181), calls=%async_computation.8 | async-start | bytes 327680 | tf_op jit(solution)/shard_map/all_to_all | solution.py:27
  169.8 8.2 %all-to-all-done.8.refs_2_ = bf16[8,16,640]{2,1,0:T(8,128)(2,1)S(1)} async-done(((bf16[8,16,640]{2,1,0:T(8,128)(2,1)}), bf16[8,16,640]{2,1,0:T(8,128)(2,1)S(1)}, u32[]{:S(2)}, u32[]{:S(2)}) %all-to-all-start.8) | async-done | bytes 163872 | tf_op jit(solution)/shard_map/all_to_all | solution.py:27
  185.4 8.5 %all-to-all-done.9.refs_1_ = bf16[8,16,640]{2,1,0:T(8,128)(2,1)S(1)} async-done(((bf16[8,16,640]{2,1,0:T(8,128)(2,1)}), bf16[8,16,640]{2,1,0:T(8,128)(2,1)S(1)}, u32[]{:S(2)}, u32[]{:S(2)}) %all-to-all-start.9) | async-done | bytes 163872 | tf_op jit(solution)/shard_map/all_to_all | solution.py:27
  196.2 11.8 %all_to_all.96.refs_1_ = bf16[8,16,640]{2,1,0:T(8,128)(2,1)S(1)} all-to-all(bf16[8,16,640]{2,1,0:T(8,128)(2,1)S(1)} %get-tuple-element.26), channel_id=1, replica_groups=mesh['z2'=2,'z1'=2,'z0'=2,'x'=4,'c'=2,'panel'=8] {'panel'}, dimensions={0} | all-to-all | bytes 327680 | tf_op jit(solution)/shard_map/all_to_all | solution.py:27
  212.2 9.0 %all-to-all-done.11.refs_1_ = bf16[8,16,640]{2,1,0:T(8,128)(2,1)S(1)} async-done(((bf16[8,16,640]{2,1,0:T(8,128)(2,1)}), bf16[8,16,640]{2,1,0:T(8,128)(2,1)S(1)}, u32[]{:S(2)}, u32[]{:S(2)}) %all-to-all-start.11) | async-done | bytes 163872 | tf_op jit(solution)/shard_map/all_to_all | solution.py:27
  223.7 8.2 %all_to_all.97.refs_0_ = bf16[4,16,640]{2,1,0:T(8,128)(2,1)S(1)} all-to-all(bf16[4,16,640]{2,1,0:T(8,128)(2,1)S(1)} %get-tuple-element.27), channel_id=1, replica_groups=mesh['z2'=2,'z1'=2,'z0'=2,'x'=4,'c'=2,'panel'=8] {'z1','z0'}, dimensions={0} | all-to-all | bytes 163840 | tf_op jit(solution)/shard_map/all_to_all | solution.py:27
  239.9 10.2 %all-to-all-done.13.refs_1_ = bf16[8,16,1280]{2,1,0:T(8,128)(2,1)S(1)} async-done(((bf16[8,16,1280]{2,1,0:T(8,128)(2,1)}), bf16[8,16,1280]{2,1,0:T(8,128)(2,1)S(1)}, u32[]{:S(2)}, u32[]{:S(2)}) %all-to-all-start.13) | async-done | bytes 327712 | tf_op jit(solution)/shard_map/all_to_all | solution.py:27
  255.0 5.8 %all-to-all-done.14.refs_1_.held_ref = bf16[4,16,1920]{2,1,0:T(8,128)(2,1)S(1)} async-done(((bf16[4,16,1920]{2,1,0:T(8,128)(2,1)}), bf16[4,16,1920]{2,1,0:T(8,128)(2,1)S(1)}, u32[]{:S(2)}, u32[]{:S(2)}) %all-to-all-start.14) | async-done | bytes 245792 | tf_op jit(solution)/shard_map/all_to_all | solution.py:27
  280.2 6.9 %all-to-all-done.15 = bf16[16,2,2560]{2,1,0:T(2,128)(2,1)S(1)} async-done(((bf16[16,2,2560]{2,1,0:T(2,128)(2,1)}), bf16[16,2,2560]{2,1,0:T(2,128)(2,1)S(1)}, u32[]{:S(2)}, u32[]{:S(2)}) %all-to-all-start.15) | async-done | bytes 163872 | tf_op jit(solution)/shard_map/all_to_all | solution.py:27
  292.3 8.3 %all-to-all-done.16 = bf16[8,2,2560]{2,1,0:T(2,128)(2,1)S(1)} async-done(((bf16[8,2,2560]{2,1,0:T(2,128)(2,1)}), bf16[8,2,2560]{2,1,0:T(2,128)(2,1)S(1)}, u32[]{:S(2)}, u32[]{:S(2)}) %all-to-all-start.16) | async-done | bytes 81952 | tf_op jit(solution)/shard_map/all_to_all | solution.py:27
  304.7 5.7 %all-to-all-start.17 = ((bf16[8,18,640]{2,1,0:T(8,128)(2,1)}), bf16[8,18,640]{2,1,0:T(8,128)(2,1)S(1)}, u32[]{:S(2)}, u32[]{:S(2)}) async-start(bf16[8,18,640]{2,1,0:T(8,128)(2,1)} %pad_maximum_fusion.2), calls=%async_computation.17 | async-start | bytes 491520 | tf_op jit(solution)/shard_map/all_to_all | solution.py:27
  310.4 5.3 %all-to-all-done.17.got_ref = bf16[8,18,640]{2,1,0:T(8,128)(2,1)S(1)} async-done(((bf16[8,18,640]{2,1,0:T(8,128)(2,1)}), bf16[8,18,640]{2,1,0:T(8,128)(2,1)S(1)}, u32[]{:S(2)}, u32[]{:S(2)}) %all-to-all-start.17) | async-done | bytes 184352 | tf_op jit(solution)/shard_map/all_to_all | solution.py:27
  324.5 6.9 %all-to-all-done.18 = bf16[8,16,640]{2,1,0:T(8,128)(2,1)S(1)} async-done(((bf16[8,16,640]{2,1,0:T(8,128)(2,1)}), bf16[8,16,640]{2,1,0:T(8,128)(2,1)S(1)}, u32[]{:S(2)}, u32[]{:S(2)}) %all-to-all-start.18) | async-done | bytes 163872 | tf_op jit(solution)/shard_map/all_to_all | solution.py:27
  (156 shorter events, 123.2 us)
Async XLA Ops:
  7.2 86.1 %all-gather.9.cloned.1.call-start = ((), (), s32[]{:S(2)}) async-start(), calls=%async_computation.19 | async-start | bytes 11059200 | tf_op jit(solution)/shard_map/all_gather | solution.py:473
  9.9 118.9 %all-gather.11.cloned.1.call-start = ((), (), s32[]{:S(2)}) async-start(), calls=%async_computation.20 | async-start | bytes 5529600 | tf_op jit(solution)/shard_map/all_gather | solution.py:473
  10.9 158.9 %all-gather.13.cloned.1.call-start = ((), (), s32[]{:S(2)}) async-start(), calls=%async_computation.21 | async-start | bytes 1843200 | tf_op jit(solution)/shard_map/all_gather | solution.py:473
  11.6 289.0 %all-gather.15.cloned.1.call-start = ((), (), s32[]{:S(2)}) async-start(), calls=%async_computation.22 | async-start | bytes 7372800 | tf_op jit(solution)/shard_map/all_gather | solution.py:473
  12.2 22.1 %collective-permute-start = (bf16[2,640,640]{2,1,0:T(8,128)(2,1)S(1)}, bf16[2,640,640]{2,1,0:T(8,128)(2,1)}, u32[]{:S(2)}, u32[]{:S(2)}) collective-permute-start(bf16[2,640,640]{2,1,0:T(8,128)(2,1)S(1)} %copy-done), channel_id=1, source_target_pairs={{0,8},{8,0},{1,9},{9,1},{2,10},{10,2},{3,11},{11,3},{4,12},{12,4},... | collective-permute-start | bytes 4915208 | tf_op jit(solution)/shard_map/ppermute | solution.py:529
  15.1 19.2 %all-to-all-start = ((bf16[16,8,1280]{2,1,0:T(8,128)(2,1)}), bf16[16,8,1280]{2,1,0:T(8,128)(2,1)S(1)}, u32[]{:S(2)}, u32[]{:S(2)}) async-start(bf16[16,8,1280]{2,1,0:T(8,128)(2,1)} %bitcast.6), calls=%async_computation | async-start | bytes 655360 | tf_op jit(solution)/shard_map/all_to_all | solution.py:27
  22.4 22.2 %collective-permute-start.1 = (bf16[2,320,640]{2,1,0:T(8,128)(2,1)S(1)}, bf16[2,320,640]{2,1,0:T(8,128)(2,1)}, u32[]{:S(2)}, u32[]{:S(2)}) collective-permute-start(bf16[2,320,640]{2,1,0:T(8,128)(2,1)S(1)} %copy-done.1), channel_id=1, source_target_pairs={{0,8},{8,0},{1,9},{9,1},{2,10},{10,2},{3,11},{11,3},{4,12},{12,4},... | collective-permute-start | bytes 2457608 | tf_op jit(solution)/shard_map/ppermute | solution.py:530
  38.4 18.6 %all-to-all-start.1 = ((bf16[4,96,640]{2,1,0:T(8,128)(2,1)}), bf16[4,96,640]{2,1,0:T(8,128)(2,1)S(1)}, u32[]{:S(2)}, u32[]{:S(2)}) async-start(bf16[4,96,640]{2,1,0:T(8,128)(2,1)} %shard_map.174), calls=%async_computation.1 | async-start | bytes 983040 | tf_op jit(solution)/shard_map/all_to_all | solution.py:27
  60.5 19.1 %all-to-all-start.2 = ((bf16[64,2,640]{2,1,0:T(2,128)(2,1)}), bf16[64,2,640]{2,1,0:T(2,128)(2,1)S(1)}, u32[]{:S(2)}, u32[]{:S(2)}) async-start(bf16[64,2,640]{2,1,0:T(2,128)(2,1)} %reshape.188), calls=%async_computation.2 | async-start | bytes 327680 | tf_op jit(solution)/shard_map/all_to_all | solution.py:27
  80.5 12.7 %all-to-all-start.3 = ((bf16[8,2,5120]{2,1,0:T(2,128)(2,1)}), bf16[8,2,5120]{2,1,0:T(2,128)(2,1)S(1)}, u32[]{:S(2)}, u32[]{:S(2)}) async-start(bf16[8,2,5120]{2,1,0:T(2,128)(2,1)} %broadcast_in_dim.109), calls=%async_computation.3 | async-start | bytes 327680 | tf_op jit(solution)/shard_map/all_to_all | solution.py:27
  97.2 5.7 %collective-permute-start.2 = (bf16[1,16,640]{2,1,0:T(8,128)(2,1)S(1)}, bf16[1,16,640]{2,1,0:T(8,128)(2,1)S(1)}, u32[]{:S(2)}, u32[]{:S(2)}) collective-permute-start(bf16[1,16,640]{2,1,0:T(8,128)(2,1)S(1)} %get-tuple-element.20.refs_1_), channel_id=1, source_target_pairs={{0,64},{64,0},{1,65},{65,1},{2,66},{66,2},{3,67},{67,3},{4,68},{68... | collective-permute-start | bytes 61448 | tf_op jit(solution)/shard_map/ppermute | solution.py:39
  106.6 14.5 %all-to-all-start.4 = ((bf16[8,16,1280]{2,1,0:T(8,128)(2,1)}), bf16[8,16,1280]{2,1,0:T(8,128)(2,1)S(1)}, u32[]{:S(2)}, u32[]{:S(2)}) async-start(bf16[8,16,1280]{2,1,0:T(8,128)(2,1)} %get-tuple-element.21), calls=%async_computation.4 | async-start | bytes 655360 | tf_op jit(solution)/shard_map/all_to_all | solution.py:27
  121.8 11.3 %all-to-all-start.5 = ((bf16[4,16,1280]{2,1,0:T(8,128)(2,1)}), bf16[4,16,1280]{2,1,0:T(8,128)(2,1)S(1)}, u32[]{:S(2)}, u32[]{:S(2)}) async-start(bf16[4,16,1280]{2,1,0:T(8,128)(2,1)} %shard_map.178), calls=%async_computation.5 | async-start | bytes 327680 | tf_op jit(solution)/shard_map/all_to_all | solution.py:27
  136.8 9.1 %all-to-all-start.6 = ((bf16[4,16,640]{2,1,0:T(8,128)(2,1)}), bf16[4,16,640]{2,1,0:T(8,128)(2,1)S(1)}, u32[]{:S(2)}, u32[]{:S(2)}) async-start(bf16[4,16,640]{2,1,0:T(8,128)(2,1)} %get-tuple-element.23), calls=%async_computation.6 | async-start | bytes 163840 | tf_op jit(solution)/shard_map/all_to_all | solution.py:27
  160.7 17.3 %all-to-all-start.8 = ((bf16[8,16,640]{2,1,0:T(8,128)(2,1)}), bf16[8,16,640]{2,1,0:T(8,128)(2,1)S(1)}, u32[]{:S(2)}, u32[]{:S(2)}) async-start(bf16[8,16,640]{2,1,0:T(8,128)(2,1)} %shard_map.181), calls=%async_computation.8 | async-start | bytes 327680 | tf_op jit(solution)/shard_map/all_to_all | solution.py:27
  181.2 12.7 %all-to-all-start.9 = ((bf16[8,16,640]{2,1,0:T(8,128)(2,1)}), bf16[8,16,640]{2,1,0:T(8,128)(2,1)S(1)}, u32[]{:S(2)}, u32[]{:S(2)}) async-start(bf16[8,16,640]{2,1,0:T(8,128)(2,1)} %shard_map.182), calls=%async_computation.9 | async-start | bytes 327680 | tf_op jit(solution)/shard_map/all_to_all | solution.py:27
  208.7 12.5 %all-to-all-start.11 = ((bf16[8,16,640]{2,1,0:T(8,128)(2,1)}), bf16[8,16,640]{2,1,0:T(8,128)(2,1)S(1)}, u32[]{:S(2)}, u32[]{:S(2)}) async-start(bf16[8,16,640]{2,1,0:T(8,128)(2,1)} %shard_map.184), calls=%async_computation.11 | async-start | bytes 327680 | tf_op jit(solution)/shard_map/all_to_all | solution.py:27
  235.5 14.5 %all-to-all-start.13 = ((bf16[8,16,1280]{2,1,0:T(8,128)(2,1)}), bf16[8,16,1280]{2,1,0:T(8,128)(2,1)S(1)}, u32[]{:S(2)}, u32[]{:S(2)}) async-start(bf16[8,16,1280]{2,1,0:T(8,128)(2,1)} %shard_map.186), calls=%async_computation.13 | async-start | bytes 655360 | tf_op jit(solution)/shard_map/all_to_all | solution.py:27
  250.8 10.0 %all-to-all-start.14 = ((bf16[4,16,1920]{2,1,0:T(8,128)(2,1)}), bf16[4,16,1920]{2,1,0:T(8,128)(2,1)S(1)}, u32[]{:S(2)}, u32[]{:S(2)}) async-start(bf16[4,16,1920]{2,1,0:T(8,128)(2,1)} %shard_map.187), calls=%async_computation.14 | async-start | bytes 491520 | tf_op jit(solution)/shard_map/all_to_all | solution.py:27
  264.1 5.7 %collective-permute-start.3 = (bf16[1,16,640]{2,1,0:T(8,128)(2,1)S(1)}, bf16[1,16,640]{2,1,0:T(8,128)(2,1)S(1)}, u32[]{:S(2)}, u32[]{:S(2)}) collective-permute-start(bf16[1,16,640]{2,1,0:T(8,128)(2,1)S(1)} %get-tuple-element.30.refs_0_), channel_id=1, source_target_pairs={{0,64},{64,0},{1,65},{65,1},{2,66},{66,2},{3,67},{67,3},{4,68},{68... | collective-permute-start | bytes 61448 | tf_op jit(solution)/shard_map/ppermute | solution.py:39
  275.0 12.1 %all-to-all-start.15 = ((bf16[16,2,2560]{2,1,0:T(2,128)(2,1)}), bf16[16,2,2560]{2,1,0:T(2,128)(2,1)S(1)}, u32[]{:S(2)}, u32[]{:S(2)}) async-start(bf16[16,2,2560]{2,1,0:T(2,128)(2,1)} %pad_maximum_fusion.3), calls=%async_computation.15 | async-start | bytes 327680 | tf_op jit(solution)/shard_map/all_to_all | solution.py:27
  288.7 11.9 %all-to-all-start.16 = ((bf16[8,2,2560]{2,1,0:T(2,128)(2,1)}), bf16[8,2,2560]{2,1,0:T(2,128)(2,1)S(1)}, u32[]{:S(2)}, u32[]{:S(2)}) async-start(bf16[8,2,2560]{2,1,0:T(2,128)(2,1)} %broadcast_in_dim.110), calls=%async_computation.16 | async-start | bytes 163840 | tf_op jit(solution)/shard_map/all_to_all | solution.py:27
  304.7 11.0 %all-to-all-start.17 = ((bf16[8,18,640]{2,1,0:T(8,128)(2,1)}), bf16[8,18,640]{2,1,0:T(8,128)(2,1)S(1)}, u32[]{:S(2)}, u32[]{:S(2)}) async-start(bf16[8,18,640]{2,1,0:T(8,128)(2,1)} %pad_maximum_fusion.2), calls=%async_computation.17 | async-start | bytes 491520 | tf_op jit(solution)/shard_map/all_to_all | solution.py:27
  318.4 13.0 %all-to-all-start.18 = ((bf16[8,16,640]{2,1,0:T(8,128)(2,1)}), bf16[8,16,640]{2,1,0:T(8,128)(2,1)S(1)}, u32[]{:S(2)}, u32[]{:S(2)}) async-start(bf16[8,16,640]{2,1,0:T(8,128)(2,1)} %bitcast.48), calls=%async_computation.18 | async-start | bytes 327680 | tf_op jit(solution)/shard_map/all_to_all | solution.py:27
  (11 other events, 99.0 us)
Sparse Core Ops, SparseCore 0:
  10.1 70.8 all-gather.8
  83.1 40.7 all-gather.10
  126.1 30.3 all-gather.12
  158.4 47.0 all-gather.14
